TPU v7x, 128 devices: a whole 4x4x4 slice. The times are simulated.
128 devices in a mesh: dp: 8 (over y, core), space: 16 (over x, z).
Axes of the slice: x: 4, y: 4, z: 4, core: 2. Of those that a mesh axis runs over, the one named last changes fastest.
Arguments:
- activations: bfloat16 [2, 8, 8, 32, 32, 768], P(None, 'dp', None, 'space'), may hold values from -60 to 60
- out_grads: bfloat16 [2, 8, 8, 32, 32, 768], P(None, 'dp', None, 'space'), may hold values from -6 to 6
- omega: bfloat16 [768, 128], replicated, may hold values from -0.21875 to 0.21875
Outputs:
- basis: float32 [2, 20736, 128], P(None, ('dp', 'space'))
All inputs are finite; a program needn't handle non-finite values.
Results may differ from a plain program's by a relative error of at most 0.0033.
Values may be sent and summed in bfloat16 or wider, within the bound.
A program may use at most 128 MiB of HBM per device.

v0:
```python
import math

import jax
import jax.numpy as jnp
from jax import lax
from jax.sharding import PartitionSpec as P


def with_halo(value, sides, width):
    for axis, dim in sides:
        count, length = (lax.axis_size(axis), value.shape[dim])
        up = [(i, (i + 1) % count) for i in range(count - 1)]
        down = [(j, i) for i, j in up]
        last = lax.slice_in_dim(value, length - width, length, axis=dim)
        initial = lax.slice_in_dim(value, 0, width, axis=dim)
        before = lax.ppermute(last, axis, up)
        after = lax.ppermute(initial, axis, down)
        value = jnp.concatenate([before, value, after], axis=dim)
    return value


def solve_layer(lower, block_rows):
    return jax.scipy.linalg.solve_triangular(lower, block_rows.T, lower=True).T


def shards(activations, out_grads, omega):
    layer_count, clips, frames, height, widths, channels = activations.shape
    rank_cols = omega.shape[1]
    grads_flat = out_grads.reshape(-1, channels)
    sketched = jnp.dot(grads_flat, omega, preferred_element_type=jnp.float32).astype(jnp.bfloat16)
    sketched = sketched.reshape(layer_count, clips, frames, height, widths, rank_cols)
    padding = ((0, 0), (0, 0), (1, 1), (0, 0), (1, 1), (0, 0))
    per_layer = []
    extended = with_halo(activations, (("space", 3),), 1)
    extended = jnp.pad(extended, padding)
    for layer in range(layer_count):
        sketch_flat = sketched[layer].reshape(-1, rank_cols)
        blocks = []
        for along_t in range(3):
            for along_h in range(3):
                for along_w in range(3):
                    window = extended[
                        layer,
                        :,
                        along_t : along_t + frames,
                        along_h : along_h + height,
                        along_w : along_w + widths,
                        :,
                    ]
                    window = window.reshape(-1, channels)
                    blocks.append(
                        jnp.einsum(
                            "nc,nr->cr", window, sketch_flat, preferred_element_type=jnp.float32
                        )
                    )
        per_layer.append(jnp.concatenate(blocks, axis=0))
    partial_sketch = jnp.stack(per_layer)
    rows_block = lax.psum_scatter(partial_sketch, ("dp", "space"), scatter_dimension=1, tiled=True)
    gram_local = jnp.einsum("lnr,lns->lrs", rows_block, rows_block, precision=lax.Precision.HIGHEST)
    total = lax.psum(gram_local, ("dp", "space"))
    lower = jnp.linalg.cholesky(total)
    basis = jax.vmap(solve_layer)(lower, rows_block)
    return basis * math.sqrt(27 * channels)


def solution(mesh):
    return jax.shard_map(
        shards,
        mesh=mesh,
        in_specs=(
            P(None, "dp", None, "space", None, None),
            P(None, "dp", None, "space", None, None),
            P(),
        ),
        out_specs=P(None, ("dp", "space"), None),
        check_vma=False,
    )
```

profile of v0, /device:TPU:1, one launch (start us, length us, event | category | flops | bytes accessed | tf_op | source)
XLA Modules:
  0.0 591.8 jit_solution(6991327226084615586)
XLA Ops:
  6.5 1.6 fusion.73
  8.1 4.4 collective-permute-start
  12.6 1.3 collective-permute-start.1
  13.9 1.5 convolution_convert_fusion
  15.4 1.5 fusion.72
  16.9 11.8 %collective-permute-done = bf16[2,1,8,1,32,768]{5,4,3,2,1,0:T(8,128)(2,1)S(1)} collective-permute-done((bf16[2,1,8,1,32,768]{5,4,3,2,1,0:T(8,128)(2,1)S(1)}, bf16[2,1,8,1,32,768]{5,4,3,2,1,0:T(8,128)(2,1)S(1)}, u32[]{:S(2)}, u32[]{:S(2)}) %collective-permute-start) | collective-permute-done | bytes 786464 | tf_op jit(solution)/shard_map/ppermute | solution.py:16
  28.7 4.1 collective-permute-done.1
  32.8 3.8 select_maximum_fusion
  36.7 3.8 fusion.69
  40.5 6.9 %fusion.68 = (bf16[1,1,8,2,32,768]{5,4,3,2,1,0:T(8,128)(2,1)}, bf16[1,1,8,2,32,768]{5,4,3,2,1,0:T(8,128)(2,1)S(1)}, bf16[1,1,8,2,32,768]{5,4,3,2,1,0:T(8,128)(2,...) fusion(bf16[2,1,10,4,34,768]{5,4,3,2,1,0:T(8,128)(2,1)S(1)} %se, ...), kind=kLoop, calls=%fused_computation.142 | loop fusion | bytes 29884416 | tf_op jit(solution)/shard_map/slice | solution.py:42
  47.3 5.7 fusion.67
  53.1 1.3 constant_dynamic-update-slice_fusion.1
  55.1 1.7 constant_dynamic-update-slice_fusion.2
  62.1 1.6 convolution_dynamic-update-slice_fusion.40
  63.8 1.6 convolution_dynamic-update-slice_fusion.39
  65.4 0.4 fusion.7
  68.0 0.4 convolution_dynamic-update-slice_fusion.33
  68.4 0.4 convolution_dynamic-update-slice_fusion.32
  68.9 0.4 convolution_dynamic-update-slice_fusion.31
  69.3 0.4 convolution_dynamic-update-slice_fusion.30
  69.7 0.4 convolution_dynamic-update-slice_fusion.29
  70.1 0.4 convolution_dynamic-update-slice_fusion.28
  70.6 0.4 convolution_dynamic-update-slice_fusion.27
  71.0 0.4 convolution_dynamic-update-slice_fusion.26
  71.9 0.4 convolution_dynamic-update-slice_fusion.23
  72.3 0.6 convolution_dynamic-update-slice_fusion.22
  73.7 0.4 convolution_dynamic-update-slice_fusion.19
  74.1 0.4 convolution_dynamic-update-slice_fusion.18
  75.4 0.4 convolution_dynamic-update-slice_fusion.15
  75.8 0.4 convolution_dynamic-update-slice_fusion.14
  76.7 0.5 fusion.6
  78.8 0.4 convolution_dynamic-update-slice_fusion.8
  79.2 0.4 convolution_dynamic-update-slice_fusion.7
  80.5 0.4 convolution_dynamic-update-slice_fusion.4
  80.9 0.4 convolution_dynamic-update-slice_fusion.3
  82.1 0.4 convolution_dynamic-update-slice_fusion
  82.6 5.9 pad_maximum_fusion
  88.4 78.2 %copy.22 = f32[2,20736,128]{2,0,1:T(2,128)} copy(f32[2,20736,128]{2,1,0:T(8,128)S(1)} %pad_maximum_fusion) | data formatting | bytes 42467328 | tf_op jit(solution)/shard_map/stack | solution.py:57
  166.7 228.6 %all-reduce.7.cloned.1.call-done = f32[2,20736,128]{2,0,1:T(2,128)} async-done(((f32[2,20736,128]{2,0,1:T(2,128)}), f32[2,20736,128]{2,0,1:T(2,128)}) %all-reduce.7.cloned.1.call-update) | async-done | bytes 21233680
  395.3 0.9 constant_dynamic-slice_fusion
  396.2 1.3 fusion.8
  397.6 140.7 %all-reduce.5.cloned.1.call-done = f32[2,128,128]{1,2,0:T(8,128)} async-done(((f32[2,128,128]{1,2,0:T(8,128)}), f32[2,128,128]{1,2,0:T(8,128)}) %all-reduce.5.cloned.1.call-update) | async-done | bytes 131088 | tf_op jit(solution)/shard_map/psum | solution.py:60
  538.3 1.0 copy.26
  539.3 0.9 fusion.12
  540.2 23.5 %custom-call.8 = f32[2,128,128]{2,1,0:T(8,128)S(1)} custom-call(f32[2,128,128]{2,1,0:T(8,128)S(1)} %fusion.12), custom_call_target="Cholesky" | custom-call | tf_op jit(solution)/shard_map/jit(cholesky)/cholesky | solution.py:61
  563.9 19.7 %custom-call.9 = f32[2,1,128,128]{2,3,1,0:T(8,128)S(1)} custom-call(f32[2,1,128,128]{3,2,1,0:T(8,128)S(1)} %select_bitcast_fusion), custom_call_target="InvertDiagBlocksLowerTriangular" | custom-call | tf_op jit(solution)/shard_map/vmap(jit(_solve_triangular))/triangular_solve | solution.py:23
  583.6 0.4 convolution_multiply_fusion
  584.0 0.8 copy.29
  (107 shorter events, 13.9 us)
Async XLA Ops:
  6.5 7.3 %copy-start = (bf16[2,1,8,2,32,768]{5,4,3,2,1,0:T(8,128)(2,1)S(1)}, bf16[2,1,8,2,32,768]{5,4,3,2,1,0:T(8,128)(2,1)}, u32[]{:S(2)}) copy-start(bf16[2,1,8,2,32,768]{5,4,3,2,1,0:T(8,128)(2,1)} %param.4) | copy-start | bytes 4718596
  6.5 388.8 %all-reduce.7.cloned.1.call-start = ((), (), s32[]{:S(2)}) async-start(), calls=%async_computation.1 | async-start | bytes 42467328
  8.1 20.6 %collective-permute-start = (bf16[2,1,8,1,32,768]{5,4,3,2,1,0:T(8,128)(2,1)S(1)}, bf16[2,1,8,1,32,768]{5,4,3,2,1,0:T(8,128)(2,1)S(1)}, u32[]{:S(2)}, u32[]{:S(2)}) collective-permute-start(bf16[2,1,8,1,32,768]{5,4,3,2,1,0:T(8,128)(2,1)S(1)} %get-tuple-element.61), channel_id=1, source_target_pairs={{0,1},{1,2},{2,3},{3,4},{4,5},{5,6},{6,7},{7,8},{8,9},{9,10},{10,1... | collective-permute-start | bytes 2359304 | tf_op jit(solution)/shard_map/ppermute | solution.py:16
  12.6 20.3 %collective-permute-start.1 = (bf16[2,1,8,1,32,768]{5,4,3,2,1,0:T(8,128)(2,1)S(1)}, bf16[2,1,8,1,32,768]{5,4,3,2,1,0:T(8,128)(2,1)S(1)}, u32[]{:S(2)}, u32[]{:S(2)}) collective-permute-start(bf16[2,1,8,1,32,768]{5,4,3,2,1,0:T(8,128)(2,1)S(1)} %get-tuple-element.62), channel_id=1, source_target_pairs={{1,0},{2,1},{3,2},{4,3},{5,4},{6,5},{7,6},{8,7},{9,8},{10,9},{11,1... | collective-permute-start | bytes 2359304 | tf_op jit(solution)/shard_map/ppermute | solution.py:17
  28.7 11.8 %copy-start.29 = (bf16[2,1,8,1,32,768]{5,4,3,2,1,0:T(8,128)(2,1)}, bf16[2,1,8,1,32,768]{5,4,3,2,1,0:T(8,128)(2,1)S(1)}, u32[]{:S(2)}) copy-start(bf16[2,1,8,1,32,768]{5,4,3,2,1,0:T(8,128)(2,1)S(1)} %collective-permute-done) | copy-start | bytes 2359300
  32.8 7.6 %copy-start.25 = (bf16[2,1,8,1,32,768]{5,4,3,2,1,0:T(8,128)(2,1)}, bf16[2,1,8,1,32,768]{5,4,3,2,1,0:T(8,128)(2,1)S(1)}, u32[]{:S(2)}) copy-start(bf16[2,1,8,1,32,768]{5,4,3,2,1,0:T(8,128)(2,1)S(1)} %collective-permute-done.1) | copy-start | bytes 2359300
  47.3 7.1 %copy-start.2 = (bf16[2,1,8,2,32,768]{5,4,3,2,1,0:T(8,128)(2,1)S(1)}, bf16[2,1,8,2,32,768]{5,4,3,2,1,0:T(8,128)(2,1)}, u32[]{:S(2)}) copy-start(bf16[2,1,8,2,32,768]{5,4,3,2,1,0:T(8,128)(2,1)} %param.3) | copy-start | bytes 4718596
  53.0 3.9 copy-start.30
  53.1 4.3 copy-start.31
  53.1 4.7 copy-start.28
  53.1 5.1 copy-start.27
  53.1 5.6 copy-start.26
  53.1 6.0 %copy-start.24 = (bf16[1,1,8,2,32,768]{5,4,3,2,1,0:T(8,128)(2,1)S(1)}, bf16[1,1,8,2,32,768]{5,4,3,2,1,0:T(8,128)(2,1)}, u32[]{:S(2)}) copy-start(bf16[1,1,8,2,32,768]{5,4,3,2,1,0:T(8,128)(2,1)} %get-tuple-element.47) | copy-start | bytes 2359300
  54.5 5.1 copy-start.23
  54.5 5.5 copy-start.22
  54.5 5.9 copy-start.21
  54.9 5.9 %copy-start.19 = (bf16[1,1,8,2,32,768]{5,4,3,2,1,0:T(8,128)(2,1)S(1)}, bf16[1,1,8,2,32,768]{5,4,3,2,1,0:T(8,128)(2,1)}, u32[]{:S(2)}) copy-start(bf16[1,1,8,2,32,768]{5,4,3,2,1,0:T(8,128)(2,1)} %get-tuple-element.43) | copy-start | bytes 2359300
  54.9 6.4 %copy-start.20 = (bf16[1,1,8,2,32,768]{5,4,3,2,1,0:T(8,128)(2,1)S(1)}, bf16[1,1,8,2,32,768]{5,4,3,2,1,0:T(8,128)(2,1)}, u32[]{:S(2)}) copy-start(bf16[1,1,8,2,32,768]{5,4,3,2,1,0:T(8,128)(2,1)} %get-tuple-element.42) | copy-start | bytes 2359300
  56.9 9.0 %copy-start.18 = (bf16[1,1,8,2,32,768]{5,4,3,2,1,0:T(8,128)(2,1)S(1)}, bf16[1,1,8,2,32,768]{5,4,3,2,1,0:T(8,128)(2,1)}, u32[]{:S(2)}) copy-start(bf16[1,1,8,2,32,768]{5,4,3,2,1,0:T(8,128)(2,1)} %get-tuple-element.39) | copy-start | bytes 2359300
  56.9 9.4 %copy-start.17 = (bf16[1,1,8,2,32,768]{5,4,3,2,1,0:T(8,128)(2,1)S(1)}, bf16[1,1,8,2,32,768]{5,4,3,2,1,0:T(8,128)(2,1)}, u32[]{:S(2)}) copy-start(bf16[1,1,8,2,32,768]{5,4,3,2,1,0:T(8,128)(2,1)} %get-tuple-element.38) | copy-start | bytes 2359300
  57.8 9.4 %copy-start.16 = (bf16[1,1,8,2,32,768]{5,4,3,2,1,0:T(8,128)(2,1)S(1)}, bf16[1,1,8,2,32,768]{5,4,3,2,1,0:T(8,128)(2,1)}, u32[]{:S(2)}) copy-start(bf16[1,1,8,2,32,768]{5,4,3,2,1,0:T(8,128)(2,1)} %get-tuple-element.37) | copy-start | bytes 2359300
  58.2 9.4 %copy-start.15 = (bf16[1,1,8,2,32,768]{5,4,3,2,1,0:T(8,128)(2,1)S(1)}, bf16[1,1,8,2,32,768]{5,4,3,2,1,0:T(8,128)(2,1)}, u32[]{:S(2)}) copy-start(bf16[1,1,8,2,32,768]{5,4,3,2,1,0:T(8,128)(2,1)} %get-tuple-element.36) | copy-start | bytes 2359300
  58.6 9.4 %copy-start.14 = (bf16[1,1,8,2,32,768]{5,4,3,2,1,0:T(8,128)(2,1)S(1)}, bf16[1,1,8,2,32,768]{5,4,3,2,1,0:T(8,128)(2,1)}, u32[]{:S(2)}) copy-start(bf16[1,1,8,2,32,768]{5,4,3,2,1,0:T(8,128)(2,1)} %get-tuple-element.35) | copy-start | bytes 2359300
  59.1 9.3 %copy-start.13 = (bf16[1,1,8,2,32,768]{5,4,3,2,1,0:T(8,128)(2,1)S(1)}, bf16[1,1,8,2,32,768]{5,4,3,2,1,0:T(8,128)(2,1)}, u32[]{:S(2)}) copy-start(bf16[1,1,8,2,32,768]{5,4,3,2,1,0:T(8,128)(2,1)} %get-tuple-element.34) | copy-start | bytes 2359300
  59.5 9.3 %copy-start.12 = (bf16[1,1,8,2,32,768]{5,4,3,2,1,0:T(8,128)(2,1)S(1)}, bf16[1,1,8,2,32,768]{5,4,3,2,1,0:T(8,128)(2,1)}, u32[]{:S(2)}) copy-start(bf16[1,1,8,2,32,768]{5,4,3,2,1,0:T(8,128)(2,1)} %get-tuple-element.33) | copy-start | bytes 2359300
  59.9 9.3 %copy-start.11 = (bf16[1,1,8,2,32,768]{5,4,3,2,1,0:T(8,128)(2,1)S(1)}, bf16[1,1,8,2,32,768]{5,4,3,2,1,0:T(8,128)(2,1)}, u32[]{:S(2)}) copy-start(bf16[1,1,8,2,32,768]{5,4,3,2,1,0:T(8,128)(2,1)} %get-tuple-element.32) | copy-start | bytes 2359300
  60.4 9.3 %copy-start.10 = (bf16[1,1,8,2,32,768]{5,4,3,2,1,0:T(8,128)(2,1)S(1)}, bf16[1,1,8,2,32,768]{5,4,3,2,1,0:T(8,128)(2,1)}, u32[]{:S(2)}) copy-start(bf16[1,1,8,2,32,768]{5,4,3,2,1,0:T(8,128)(2,1)} %get-tuple-element.31) | copy-start | bytes 2359300
  60.8 9.3 %copy-start.8 = (bf16[1,1,8,2,32,768]{5,4,3,2,1,0:T(8,128)(2,1)S(1)}, bf16[1,1,8,2,32,768]{5,4,3,2,1,0:T(8,128)(2,1)}, u32[]{:S(2)}) copy-start(bf16[1,1,8,2,32,768]{5,4,3,2,1,0:T(8,128)(2,1)} %get-tuple-element.30) | copy-start | bytes 2359300
  61.3 9.3 %copy-start.7 = (bf16[1,1,8,2,32,768]{5,4,3,2,1,0:T(8,128)(2,1)S(1)}, bf16[1,1,8,2,32,768]{5,4,3,2,1,0:T(8,128)(2,1)}, u32[]{:S(2)}) copy-start(bf16[1,1,8,2,32,768]{5,4,3,2,1,0:T(8,128)(2,1)} %get-tuple-element.24) | copy-start | bytes 2359300
  61.7 9.3 %copy-start.9 = (bf16[1,1,8,2,32,768]{5,4,3,2,1,0:T(8,128)(2,1)S(1)}, bf16[1,1,8,2,32,768]{5,4,3,2,1,0:T(8,128)(2,1)}, u32[]{:S(2)}) copy-start(bf16[1,1,8,2,32,768]{5,4,3,2,1,0:T(8,128)(2,1)} %get-tuple-element.5) | copy-start | bytes 2359300
  62.1 9.3 %copy-start.6 = (bf16[1,1,8,2,32,768]{5,4,3,2,1,0:T(8,128)(2,1)S(1)}, bf16[1,1,8,2,32,768]{5,4,3,2,1,0:T(8,128)(2,1)}, u32[]{:S(2)}) copy-start(bf16[1,1,8,2,32,768]{5,4,3,2,1,0:T(8,128)(2,1)} %get-tuple-element.28) | copy-start | bytes 2359300
  63.8 8.1 %copy-start.5 = (bf16[1,1,8,2,32,768]{5,4,3,2,1,0:T(8,128)(2,1)S(1)}, bf16[1,1,8,2,32,768]{5,4,3,2,1,0:T(8,128)(2,1)}, u32[]{:S(2)}) copy-start(bf16[1,1,8,2,32,768]{5,4,3,2,1,0:T(8,128)(2,1)} %get-tuple-element.27) | copy-start | bytes 2359300
  65.4 6.9 %copy-start.4 = (bf16[1,1,8,2,32,768]{5,4,3,2,1,0:T(8,128)(2,1)S(1)}, bf16[1,1,8,2,32,768]{5,4,3,2,1,0:T(8,128)(2,1)}, u32[]{:S(2)}) copy-start(bf16[1,1,8,2,32,768]{5,4,3,2,1,0:T(8,128)(2,1)} %get-tuple-element.26) | copy-start | bytes 2359300
  71.4 11.1 %copy-start.3 = (f32[20736,128]{1,0:T(8,128)}, f32[20736,128]{1,0:T(8,128)S(1)}, u32[]{:S(2)}) copy-start(f32[20736,128]{1,0:T(8,128)S(1)} %convolution_dynamic-update-slice_fusion.26) | copy-start | bytes 31850500
  166.6 418.2 %copy-start.1 = (bf16[2,1,8,2,32,768]{5,4,3,2,1,0:T(8,128)(2,1)S(1)}, bf16[2,1,8,2,32,768]{5,4,3,2,1,0:T(8,128)(2,1)}, u32[]{:S(2)}) copy-start(bf16[2,1,8,2,32,768]{5,4,3,2,1,0:T(8,128)(2,1)} %param.4) | copy-start | bytes 4718596
  166.6 371.6 %all-reduce.5.cloned.1.call-start = ((), (), s32[]{:S(2)}) async-start(), calls=%async_computation | async-start | bytes 262144 | tf_op jit(solution)/shard_map/psum | solution.py:60
Sparse Core Ops, SparseCore 0:
  166.8 228.4 all-reduce.6
  400.0 138.1 all-reduce.4
where the time goes:
time: 597 us; the launch traced here: 592 us
  waiting for transfers between devices  385 us (64%)
  local copies, waits for them, and re-layouts  104 us (17%)
  other arithmetic  54 us (9%)
  matrix products  28.2 us (5%)
  between operations  14.5 us (2%)
    unnamed x3, waiting for transfers between devices  229 us
    psum x1, waiting for transfers between devices, shards(): total = lax.psum(gram_local, ('dp', 'space'))  141 us
    another operation x1, local copies, waits for them, and re-layouts, shards(): partial_sketch = jnp.stack(per_layer)  78.2 us
    dot_general x54, matrix products, shards(): jnp.einsum('nc,nr->cr', window, sketch_flat, preferred_element_type=jnp.f...  25 us
    another operation x4, other arithmetic, shards(): lower = jnp.linalg.cholesky(total)  23.6 us
    another operation x3, other arithmetic, solve_layer(): return jax.scipy.linalg.solve_triangular(lower, block_rows.T, lower=True).T  19.8 us
    slice x6, local copies, waits for them, and re-layouts, shards(): extended[layer, :, along_t:along_t + frames, along_h:along_h + height, al...  18.1 us
  transfers between devices with their start and end apart: 4, of which 4 were waited for; matrix products, arithmetic and copies ran while one was open for 1% of the time, Pallas kernels for 0%

commit v1 on v0

v1 whole, which is shorter than its diff:
```python
import functools
import math

import jax
import jax.numpy as jnp
from jax import lax
from jax.experimental import pallas as pl
from jax.experimental.pallas import tpu as pltpu
from jax.sharding import PartitionSpec as P

MESH = pl.DeviceIdType.MESH
BF16, F32 = jnp.bfloat16, jnp.float32
HIGHEST = lax.Precision.HIGHEST
RING = 4
OWN = 162
WIN = 176
BLOCK = OWN * 16
SLAB = 6
ORDER = (2, 1, 3, 0)
CHUNKS = [(r, l) for r in ORDER for l in (0, 1)]
PANEL = 8
STAGE2 = BF16


def reduce_kernel(
    act, grads, omega, rows_out, gram_out,
    act2, act_t, sk, ext, slab, send1, recv1, send2, recv2, part1,
    send3, recv3, send4, recv4, part2, recv5,
    gram, half, recv6, recv7, ssem, rsem,
):
    layers, _, frames, height, width, channels = act.shape
    rank = omega.shape[1]
    dp, space = lax.axis_index("dp"), lax.axis_index("space")
    y, core = dp // 2, dp % 2
    x, z = space // RING, space % RING
    other_dp = y * 2 + 1 - core

    def along(axis, step):
        if axis == "x":
            return {"dp": dp, "space": (x + step) % RING * RING + z}
        if axis == "z":
            return {"dp": dp, "space": x * RING + (z + step) % RING}
        return {"dp": (y + step) % RING * 2 + core, "space": space}

    partner = {"dp": other_dp, "space": space}
    spaces = RING * RING
    below, above = (space + 1) % spaces, (space + spaces - 1) % spaces
    halo = [
        {"dp": to, "space": at} for at in (below, above) for to in (dp, other_dp)
    ]
    peers = [partner] + halo + [along(a, j) for a in ("x", "y", "z") for j in (1, 2, 3)]

    barrier = pltpu.get_barrier_semaphore()
    for peer in peers:
        pl.semaphore_signal(barrier, inc=1, device_id=peer, device_id_type=MESH)
    pl.semaphore_wait(barrier, len(peers))

    sent = []

    def send(src, dst, to):
        at = len(sent)
        copy = pltpu.make_async_remote_copy(
            src_ref=src, dst_ref=dst, send_sem=ssem.at[at], recv_sem=rsem.at[at],
            device_id=to, device_id_type=MESH,
        )
        copy.start()
        sent.append(copy)
        return copy

    act_copies, sk_copies = [], []
    for l in range(layers):
        for h in range(height):
            flat = grads[l, 0, :, h].reshape(frames * width, channels)
            value = jnp.dot(flat, omega[...], preferred_element_type=F32).astype(BF16)
            sk[l, 0, 1 + h] = value.reshape(frames, width, rank)
        copies = []
        for slot, to in ((0, 0), (1, 1)):
            copies.append(send(sk.at[l, 0, height], sk.at[l, slot, 0], halo[to]))
            copies.append(send(sk.at[l, 0, 1], sk.at[l, slot, height + 1], halo[2 + to]))
        copies.append(send(sk.at[l, 0, 1:1 + height], sk.at[l, 1, 1:1 + height], partner))
        sk_copies.append(copies)
        act_copies.append(send(act.at[l], act2.at[l], partner))

    def transpose(l, slot, source):
        for h in range(height):
            flat = source[l, 0, :, h].reshape(frames * width, channels)
            at = (slot * height + h) * frames * width
            act_t[l, :, at:at + frames * width] = flat.T

    for l in range(layers):
        transpose(l, 0, act)

    column = lax.broadcasted_iota(jnp.int32, (frames * width, rank), 0) % width
    for l in range(layers):
        for copy in sk_copies[l]:
            copy.wait_recv()
        for slot in range(2):
            for h in range(height + 2):
                value = sk[l, slot, h].reshape(frames * width, rank).astype(F32)
                if h == 0:
                    value = jnp.where(space > 0, value, 0.0)
                if h == height + 1:
                    value = jnp.where(space < spaces - 1, value, 0.0)
                ahead = jnp.where(column < width - 1, pltpu.roll(value, frames * width - 1, 0), 0.0)
                behind = jnp.where(column > 0, pltpu.roll(value, 1, 0), 0.0)
                for c, shifted in enumerate((ahead, value, behind)):
                    zero = jnp.zeros((width, rank), BF16)
                    ext[l, c, slot, h, 0] = zero
                    ext[l, c, slot, h, frames + 1] = zero
                    ext[l, c, slot, h, 1:1 + frames] = shifted.astype(BF16).reshape(frames, width, rank)
        act_copies[l].wait_recv()
        transpose(l, 1, act2)

    depth = 2 * height * frames * width

    def compute(n, r, l):
        owner = (y + r) % RING * 2 + core
        first = 27 * owner // 8

        def columns(k):
            k = jnp.minimum(first + k, 26)
            a, b, c = k // 9, k // 3 % 3, k % 3
            return ext[l, c, :, pl.ds(2 - b, height), pl.ds(2 - a, frames)].reshape(depth, rank)

        def pair(i, _):
            both = jnp.concatenate([columns(2 * i), columns(2 * i + 1)], axis=1)
            for m in range(3):
                rows = channels // 3
                value = jnp.dot(act_t[l, m * rows:(m + 1) * rows], both, preferred_element_type=F32)
                for s in range(2):
                    at = pl.multiple_of((2 * i + s) * channels + m * rows, rows)
                    slab[n, pl.ds(at, rows)] = value[:, s * rank:(s + 1) * rank]
            return 0

        lax.fori_loop(0, SLAB // 2, pair, 0)

    def window(n, r, l, mine, other):
        owner = (y + r) % RING * 2 + core
        place = mine * RING + other if l == 0 else other * RING + mine
        at = 27 * owner % 8 * (channels // 8) + OWN * place // 16 * 16
        return slab[n, pl.ds(pl.multiple_of(at, 16), WIN)]

    first_axis = ("x", "z")
    last_axis = ("z", "x")
    first_at = (x, z)
    last_at = (z, x)
    half1 = RING // 2
    step1, step2, step3, step4, step5 = {}, {}, {}, {}, {}

    def start1(n):
        r, l = CHUNKS[n]
        for o in range(RING):
            send1[n, o] = window(n, r, l, (first_at[l] + 2) % RING, o).astype(BF16)
        step1[n] = [
            send(send1.at[n, :half1], recv1.at[n, :half1], along(first_axis[l], 1)),
            send(send1.at[n, half1:], recv1.at[n, half1:], along(first_axis[l], 3)),
        ]

    def start2(n):
        r, l = CHUNKS[n]
        copies = []
        for s, step in enumerate((1, 3)):
            step1[n][s].wait_recv()
            for o in range(RING):
                value = window(n, r, l, (first_at[l] + step) % RING, o)
                if (o < half1) == (s == 0):
                    value = value + recv1[n, o].astype(F32)
                send2[n, s, o] = value.astype(BF16)
            copies.append(send(send2.at[n, s], recv2.at[n, s], along(first_axis[l], step)))
        step2[n] = copies

    def finish1(n):
        r, l = CHUNKS[n]
        for copy in step2[n]:
            copy.wait_recv()
        if r in (1, 3):
            step3[l][0 if r == 1 else 1].wait_recv()
        if r == 0:
            for copy in step4[l]:
                copy.wait_recv()
        for o in range(RING):
            value = window(n, r, l, first_at[l], o)
            value = value + recv2[n, 0, o].astype(F32) + recv2[n, 1, o].astype(F32)
            if r == 2:
                send3[l, o] = value.astype(STAGE2)
            elif r == 0:
                part2[l, o] = value + recv4[l, 0, o].astype(F32) + recv4[l, 1, o].astype(F32)
            else:
                s = 0 if r == 1 else 1
                if (o < half1) == (s == 0):
                    value = value + recv3[l, o].astype(F32)
                send4[l, s, o] = value.astype(STAGE2)
        if r == 2:
            step3[l] = [
                send(send3.at[l, :half1], recv3.at[l, :half1], along("y", 1)),
                send(send3.at[l, half1:], recv3.at[l, half1:], along("y", 3)),
            ]
        elif r == 0:
            step5[l] = [
                send(part2.at[l, (last_at[l] + j) % RING], recv5.at[l, j - 1], along(last_axis[l], j))
                for j in (1, 2, 3)
            ]
        else:
            s = 0 if r == 1 else 1
            step4.setdefault(l, []).append(send(send4.at[l, s], recv4.at[l, s], along("y", r)))

    total = len(CHUNKS)
    for n in range(total + 3):
        if n < total:
            compute(n, *CHUNKS[n])
            start1(n)
        if 1 <= n <= total:
            start2(n - 1)
        if n >= 3:
            finish1(n - 3)

    shift = 2 * space % 16
    row = lax.broadcasted_iota(jnp.int32, (WIN, rank), 0)
    for l in range(layers):
        for copy in step5[l]:
            copy.wait_recv()
        value = part2[l, last_at[l]] + recv5[l, 0] + recv5[l, 1] + recv5[l, 2]
        value = pltpu.roll(value, (WIN - shift) % WIN, 0)
        value = jnp.where(row < OWN, value, 0.0)
        rows_out[l] = value
        gram[l] = lax.dot_general(
            value, value, (((0,), (0,)), ((), ())), precision=HIGHEST, preferred_element_type=F32
        )

    part = rank // 2
    keep = pl.multiple_of(core * part, part)
    give = pl.multiple_of((1 - core) * part, part)
    copy = send(gram.at[:, pl.ds(give, part)], recv6, partner)
    copy.wait_recv()
    half[0] = gram[:, pl.ds(keep, part)] + recv6[...]
    for s, axis in enumerate(("y", "x", "z")):
        copies = [send(half.at[s], recv7.at[s, j - 1], along(axis, j)) for j in (1, 2, 3)]
        for copy in copies:
            copy.wait_recv()
        half[s + 1] = half[s] + recv7[s, 0] + recv7[s, 1] + recv7[s, 2]
    copy = send(half.at[3], gram_out.at[:, pl.ds(keep, part)], partner)
    gram_out[:, pl.ds(keep, part)] = half[3]
    copy.wait_recv()
    for copy in sent:
        copy.wait_send()


def factor_kernel(rows, gram, out, work, inverse, *, scale):
    layers, rank, _ = gram.shape
    lane = lax.broadcasted_iota(jnp.int32, (PANEL, rank), 1)
    row = lax.broadcasted_iota(jnp.int32, (PANEL, rank), 0)
    wide = lax.broadcasted_iota(jnp.int32, (rank, rank), 1)
    work[...] = gram[...]
    for p in range(rank // PANEL):
        first = p * PANEL
        for l in range(layers):
            panel = work[l, first:first + PANEL]
            cols = [
                jnp.broadcast_to(panel[:, first + j:first + j + 1], (PANEL, rank)) for j in range(PANEL)
            ]
            pivots = jnp.ones((PANEL, rank), F32)
            for j in range(PANEL):
                pivot = jnp.broadcast_to(cols[j][j:j + 1], (PANEL, rank))
                pivots = jnp.where(row == j, pivot, pivots)
                if j < PANEL - 1:
                    mult = jnp.where(row > j, cols[j] / pivot, 0.0)
                    updated = panel - mult * panel[j:j + 1]
                    panel = jnp.where((lane == first + j) & (row > j), -mult, updated)
                    for i in range(j + 1, PANEL):
                        cols[i] = cols[i] - mult * cols[i][j:j + 1]
            inside = (lane >= first) & (lane < first + PANEL)
            unit = jnp.where(lane - first < row, panel, jnp.where(lane - first == row, 1.0, 0.0))
            full = jnp.where(inside, unit, panel)
            inverse[l, first:first + PANEL] = jnp.where(lane - first <= row, full, 0.0) / jnp.sqrt(pivots)
            if first + PANEL < rank:
                step = lax.dot_general(
                    panel / pivots, full, (((0,), (0,)), ((), ())),
                    precision=HIGHEST, preferred_element_type=F32,
                )
                rest = first + PANEL
                in_wide = (wide[rest:] >= first) & (wide[rest:] < rest)
                work[l, rest:] = jnp.where(in_wide, 0.0, work[l, rest:]) - step[rest:]
    for l in range(layers):
        value = lax.dot_general(
            rows[l], inverse[l], (((1,), (1,)), ((), ())),
            precision=HIGHEST, preferred_element_type=F32,
        )
        out[l] = (value * scale)[:OWN]


def shards(activations, out_grads, omega):
    layers, clips, frames, height, width, channels = activations.shape
    rank = omega.shape[1]
    chunks = len(CHUNKS)
    vmem = pl.BlockSpec(memory_space=pltpu.VMEM)
    blocks = (RING, WIN, rank)
    rows, gram = pl.pallas_call(
        reduce_kernel,
        name="reduce",
        out_shape=(
            jax.ShapeDtypeStruct((layers, WIN, rank), F32),
            jax.ShapeDtypeStruct((layers, rank, rank), F32),
        ),
        in_specs=[vmem] * 3,
        out_specs=(vmem, vmem),
        scratch_shapes=[
            pltpu.VMEM(activations.shape, BF16),
            pltpu.VMEM((layers, channels, 2 * height * frames * width), BF16),
            pltpu.VMEM((layers, 2, height + 2, frames, width, rank), BF16),
            pltpu.VMEM((layers, 3, 2, height + 2, frames + 2, width, rank), BF16),
            pltpu.VMEM((chunks, SLAB * channels, rank), F32),
            pltpu.VMEM((chunks,) + blocks, BF16),
            pltpu.VMEM((chunks,) + blocks, BF16),
            pltpu.VMEM((chunks, 2) + blocks, BF16),
            pltpu.VMEM((chunks, 2) + blocks, BF16),
            pltpu.VMEM((8, 128), F32),
            pltpu.VMEM((layers,) + blocks, STAGE2),
            pltpu.VMEM((layers,) + blocks, STAGE2),
            pltpu.VMEM((layers, 2) + blocks, STAGE2),
            pltpu.VMEM((layers, 2) + blocks, STAGE2),
            pltpu.VMEM((layers,) + blocks, F32),
            pltpu.VMEM((layers, 3, WIN, rank), F32),
            pltpu.VMEM((layers, rank, rank), F32),
            pltpu.VMEM((4, layers, rank // 2, rank), F32),
            pltpu.VMEM((layers, rank // 2, rank), F32),
            pltpu.VMEM((3, 3, layers, rank // 2, rank), F32),
            pltpu.SemaphoreType.DMA((80,)),
            pltpu.SemaphoreType.DMA((80,)),
        ],
        compiler_params=pltpu.CompilerParams(
            collective_id=0, has_side_effects=True, vmem_limit_bytes=60 * 2**20
        ),
    )(activations, out_grads, omega)
    return pl.pallas_call(
        functools.partial(factor_kernel, scale=math.sqrt(27 * channels)),
        name="factor",
        out_shape=jax.ShapeDtypeStruct((layers, OWN, rank), F32),
        in_specs=[vmem] * 2,
        out_specs=vmem,
        scratch_shapes=[
            pltpu.VMEM((layers, rank, rank), F32),
            pltpu.VMEM((layers, rank, rank), F32),
        ],
    )(rows, gram)


def solution(mesh):
    return jax.shard_map(
        shards,
        mesh=mesh,
        in_specs=(
            P(None, "dp", None, "space", None, None),
            P(None, "dp", None, "space", None, None),
            P(),
        ),
        out_specs=P(None, ("dp", "space"), None),
        check_vma=False,
    )
```

time: 597 us -> 95.2 us (0.16)
  waiting for transfers between devices: 385 us -> 0 us
  local copies, waits for them, and re-layouts: 104 us -> 1.67 us
  Pallas kernels: 0 us -> 93.4 us
  other arithmetic: 54 us -> 0 us
  matrix products: 28.2 us -> 0 us
  between operations: 14.5 us -> 0.01 us
    unnamed x3 -> x0, waiting for transfers between devices: 229 us -> none
    psum x1 -> x0, waiting for transfers between devices: 141 us -> none  [shards(): total = lax.psum(gram_local, ('dp', 'space'))]
    pallas_call x0 -> x2, Pallas kernels: none -> 93.4 us  [the longest x1 83.9 us: shards(): pl.pallas_call(reduce_kernel, name='reduce', out_shape=(jax.ShapeDtypeStr...]
    another operation x1 -> x0, local copies, waits for them, and re-layouts: 78.2 us -> none  [shards(): partial_sketch = jnp.stack(per_layer)]
    another operation x8 -> x0, other arithmetic: 49.3 us -> none  [the longest x4 23.6 us: shards(): lower = jnp.linalg.cholesky(total)]
    dot_general x56 -> x0, matrix products: 27.8 us -> none  [the longest x54 25 us: shards(): jnp.einsum('nc,nr->cr', window, sketch_flat, preferred_element_type=jnp.f...]
    slice x7 -> x0, local copies, waits for them, and re-layouts: 19.7 us -> none  [the longest x6 18.1 us: shards(): extended[layer, :, along_t:along_t + frames, along_h:along_h + height, al...]
    ppermute x2 -> x0, waiting for transfers between devices: 15.9 us -> none  [the longest x1 11.8 us: with_halo(): before = lax.ppermute(last, axis, up)]
  transfers between devices with their start and end apart: 4 -> 0, of which waited for: 4 -> 0; matrix products, arithmetic and copies ran while one was open for 1% -> 0% of each run, Pallas kernels for 0% -> 0%
where the time goes in v1:
time: 95.2 us; the launch traced here: 95.1 us
  Pallas kernels  93.4 us (98%)
  local copies, waits for them, and re-layouts  1.67 us (2%)
    pallas_call x1, Pallas kernels, shards(): pl.pallas_call(reduce_kernel, name='reduce', out_shape=(jax.ShapeDtypeStr...  83.9 us
    pallas_call x1, Pallas kernels, shards(): pl.pallas_call(functools.partial(factor_kernel, scale=math.sqrt(27 * chan...  9.45 us

profile of v1, /device:TPU:1, one launch (start us, length us, event | category | flops | bytes accessed | tf_op | source)
XLA Modules:
  0.0 95.1 jit_solution(355063981779118972)
XLA Ops:
  0.0 83.9 %reduce.1 = (f32[2,176,128]{2,1,0:T(8,128)}, f32[2,128,128]{2,1,0:T(8,128)}) custom-call(bf16[2,1,8,2,32,768]{5,4,3,2,1,0:T(8,128)(2,1)} %act.1, bf16[2,1,8,2,32,768]{5,4,3,2,1,0:T(8,128)(2,1)} %grads.1, bf16[768,128]{1,0:T(8,128)(2,1)} %omega.1), custom_call_target="tpu_custom_call" | custom-call | tf_op jit(solution)/shard_map/reduce/pallas_call | solution.py:297
  84.0 9.5 %factor.1 = f32[2,162,128]{2,1,0:T(8,128)} custom-call(f32[2,176,128]{2,1,0:T(8,128)} %get-tuple-element.7.rows, f32[2,128,128]{2,1,0:T(8,128)} %get-tuple-element.8.gram), custom_call_target="tpu_custom_call" | custom-call | tf_op jit(solution)/shard_map/factor/pallas_call | solution.py:334
  93.4 1.7 %copy.4 = f32[2,162,128]{2,0,1:T(2,128)} copy(f32[2,162,128]{2,1,0:T(8,128)} %factor.1) | data formatting | bytes 331776 | tf_op jit(solution)/shard_map/factor/pallas_call | solution.py:334

commit v2 on v1

--- a/solution.py
+++ b/solution.py
@@ -19,16 +19,17 @@
 ORDER = (2, 1, 3, 0)
 CHUNKS = [(r, l) for r in ORDER for l in (0, 1)]
 PANEL = 8
+LAG2, LAG3 = 2, 4
 STAGE2 = BF16
 
 
 def reduce_kernel(
-    act, grads, omega, rows_out, gram_out,
-    act2, act_t, sk, ext, slab, send1, recv1, send2, recv2, part1,
+    act_in, grads_in, omega, rows_out, gram_out,
+    act, grads, act2, act_t, sk, ext, slab, send1, recv1, send2, recv2,
     send3, recv3, send4, recv4, part2, recv5,
-    gram, half, recv6, recv7, ssem, rsem,
+    gram, recv6, full, recv7, quarter, recv8, ssem, rsem, lsem,
 ):
-    layers, _, frames, height, width, channels = act.shape
+    layers, _, frames, height, width, channels = act_in.shape
     rank = omega.shape[1]
     dp, space = lax.axis_index("dp"), lax.axis_index("space")
     y, core = dp // 2, dp % 2
@@ -45,14 +46,22 @@
     partner = {"dp": other_dp, "space": space}
     spaces = RING * RING
     below, above = (space + 1) % spaces, (space + spaces - 1) % spaces
-    halo = [
-        {"dp": to, "space": at} for at in (below, above) for to in (dp, other_dp)
-    ]
+    halo = [{"dp": dp, "space": at} for at in (below, above)]
     peers = [partner] + halo + [along(a, j) for a in ("x", "y", "z") for j in (1, 2, 3)]
 
     barrier = pltpu.get_barrier_semaphore()
     for peer in peers:
         pl.semaphore_signal(barrier, inc=1, device_id=peer, device_id_type=MESH)
+
+    loads = []
+    for l in range(layers):
+        pair = [
+            pltpu.make_async_copy(grads_in.at[l], grads.at[l], lsem.at[2 * l]),
+            pltpu.make_async_copy(act_in.at[l], act.at[l], lsem.at[2 * l + 1]),
+        ]
+        for copy in pair:
+            copy.start()
+        loads.append(pair)
     pl.semaphore_wait(barrier, len(peers))
 
     sent = []
@@ -67,19 +76,19 @@
         sent.append(copy)
         return copy
 
-    act_copies, sk_copies = [], []
+    act_copies, halo_copies, row_copies = [], [], []
     for l in range(layers):
+        loads[l][0].wait()
         for h in range(height):
             flat = grads[l, 0, :, h].reshape(frames * width, channels)
             value = jnp.dot(flat, omega[...], preferred_element_type=F32).astype(BF16)
             sk[l, 0, 1 + h] = value.reshape(frames, width, rank)
-        copies = []
-        for slot, to in ((0, 0), (1, 1)):
-            copies.append(send(sk.at[l, 0, height], sk.at[l, slot, 0], halo[to]))
-            copies.append(send(sk.at[l, 0, 1], sk.at[l, slot, height + 1], halo[2 + to]))
-        copies.append(send(sk.at[l, 0, 1:1 + height], sk.at[l, 1, 1:1 + height], partner))
-        sk_copies.append(copies)
-        act_copies.append(send(act.at[l], act2.at[l], partner))
+        halo_copies.append([
+            send(sk.at[l, 0, height], sk.at[l, 0, 0], halo[0]),
+            send(sk.at[l, 0, 1], sk.at[l, 0, height + 1], halo[1]),
+        ])
+        row_copies.append(send(sk.at[l, 0, 1:1 + height], sk.at[l, 1, 1:1 + height], partner))
+        act_copies.append(send(act_in.at[l], act2.at[l], partner))
 
     def transpose(l, slot, source):
         for h in range(height):
@@ -87,29 +96,57 @@
             at = (slot * height + h) * frames * width
             act_t[l, :, at:at + frames * width] = flat.T
 
-    for l in range(layers):
+    column = lax.broadcasted_iota(jnp.int32, (frames * width, rank), 0) % width
+
+    def extend(l, slot, h):
+        value = sk[l, slot, h].reshape(frames * width, rank).astype(F32)
+        if h == 0:
+            value = jnp.where(space > 0, value, 0.0)
+        if h == height + 1:
+            value = jnp.where(space < spaces - 1, value, 0.0)
+        ahead = jnp.where(column < width - 1, pltpu.roll(value, frames * width - 1, 0), 0.0)
+        behind = jnp.where(column > 0, pltpu.roll(value, 1, 0), 0.0)
+        for c, shifted in enumerate((ahead, value, behind)):
+            zero = jnp.zeros((width, rank), BF16)
+            ext[l, c, slot, h, 0] = zero
+            ext[l, c, slot, h, frames + 1] = zero
+            ext[l, c, slot, h, 1:1 + frames] = shifted.astype(BF16).reshape(frames, width, rank)
+
+    inner, outer = range(1, 1 + height), (0, height + 1)
+
+    def prepare_own(l):
+        loads[l][1].wait()
         transpose(l, 0, act)
-
-    column = lax.broadcasted_iota(jnp.int32, (frames * width, rank), 0) % width
-    for l in range(layers):
-        for copy in sk_copies[l]:
-            copy.wait_recv()
-        for slot in range(2):
-            for h in range(height + 2):
-                value = sk[l, slot, h].reshape(frames * width, rank).astype(F32)
-                if h == 0:
-                    value = jnp.where(space > 0, value, 0.0)
-                if h == height + 1:
-                    value = jnp.where(space < spaces - 1, value, 0.0)
-                ahead = jnp.where(column < width - 1, pltpu.roll(value, frames * width - 1, 0), 0.0)
-                behind = jnp.where(column > 0, pltpu.roll(value, 1, 0), 0.0)
-                for c, shifted in enumerate((ahead, value, behind)):
-                    zero = jnp.zeros((width, rank), BF16)
-                    ext[l, c, slot, h, 0] = zero
-                    ext[l, c, slot, h, frames + 1] = zero
-                    ext[l, c, slot, h, 1:1 + frames] = shifted.astype(BF16).reshape(frames, width, rank)
+        for h in inner:
+            extend(l, 0, h)
+
+    def prepare_partner(l):
+        row_copies[l].wait_recv()
+        for h in inner:
+            extend(l, 1, h)
         act_copies[l].wait_recv()
         transpose(l, 1, act2)
+
+    relayed = []
+
+    def relay(l):
+        for copy in halo_copies[l]:
+            copy.wait_recv()
+        relayed.append([send(sk.at[l, 0, h], sk.at[l, 1, h], partner) for h in outer])
+        for h in outer:
+            extend(l, 0, h)
+
+    def prepare_edges(l):
+        for copy in relayed[l]:
+            copy.wait_recv()
+        for h in outer:
+            extend(l, 1, h)
+
+    prepare_own(0)
+    prepare_partner(0)
+    prepare_own(1)
+    relay(0)
+    prepare_edges(0)
 
     depth = 2 * height * frames * width
 
@@ -205,14 +242,18 @@
             step4.setdefault(l, []).append(send(send4.at[l, s], recv4.at[l, s], along("y", r)))
 
     total = len(CHUNKS)
-    for n in range(total + 3):
+    for n in range(total + LAG3):
+        if n == 1:
+            relay(1)
+            prepare_partner(1)
+            prepare_edges(1)
         if n < total:
             compute(n, *CHUNKS[n])
             start1(n)
-        if 1 <= n <= total:
-            start2(n - 1)
-        if n >= 3:
-            finish1(n - 3)
+        if LAG2 <= n < total + LAG2:
+            start2(n - LAG2)
+        if n >= LAG3:
+            finish1(n - LAG3)
 
     shift = 2 * space % 16
     row = lax.broadcasted_iota(jnp.int32, (WIN, rank), 0)
@@ -227,19 +268,29 @@
             value, value, (((0,), (0,)), ((), ())), precision=HIGHEST, preferred_element_type=F32
         )
 
-    part = rank // 2
-    keep = pl.multiple_of(core * part, part)
-    give = pl.multiple_of((1 - core) * part, part)
-    copy = send(gram.at[:, pl.ds(give, part)], recv6, partner)
+    copy = send(gram.at[1 - core], recv6, partner)
     copy.wait_recv()
-    half[0] = gram[:, pl.ds(keep, part)] + recv6[...]
-    for s, axis in enumerate(("y", "x", "z")):
-        copies = [send(half.at[s], recv7.at[s, j - 1], along(axis, j)) for j in (1, 2, 3)]
+    full[0] = gram[core] + recv6[...]
+    part = rank // RING
+
+    def rows_of(step):
+        return pl.ds(pl.multiple_of((y + step) % RING * part, part), part)
+
+    copies = [send(full.at[0, rows_of(j)], recv7.at[j - 1], along("y", j)) for j in (1, 2, 3)]
+    for copy in copies:
+        copy.wait_recv()
+    quarter[0] = full[0, rows_of(0)] + recv7[0] + recv7[1] + recv7[2]
+    for s, axis in enumerate(("x", "z")):
+        copies = [send(quarter.at[s], recv8.at[s, j - 1], along(axis, j)) for j in (1, 2, 3)]
         for copy in copies:
             copy.wait_recv()
-        half[s + 1] = half[s] + recv7[s, 0] + recv7[s, 1] + recv7[s, 2]
-    copy = send(half.at[3], gram_out.at[:, pl.ds(keep, part)], partner)
-    gram_out[:, pl.ds(keep, part)] = half[3]
+        quarter[s + 1] = quarter[s] + recv8[s, 0] + recv8[s, 1] + recv8[s, 2]
+    copies = [send(quarter.at[2], full.at[1, rows_of(0)], along("y", j)) for j in (1, 2, 3)]
+    full[1, rows_of(0)] = quarter[2]
+    for copy in copies:
+        copy.wait_recv()
+    copy = send(full.at[1], gram_out.at[core], partner)
+    gram_out[core] = full[1]
     copy.wait_recv()
     for copy in sent:
         copy.wait_send()
@@ -301,9 +352,11 @@
             jax.ShapeDtypeStruct((layers, WIN, rank), F32),
             jax.ShapeDtypeStruct((layers, rank, rank), F32),
         ),
-        in_specs=[vmem] * 3,
+        in_specs=[pl.BlockSpec(memory_space=pl.ANY)] * 2 + [vmem],
         out_specs=(vmem, vmem),
         scratch_shapes=[
+            pltpu.VMEM(activations.shape, BF16),
+            pltpu.VMEM(activations.shape, BF16),
             pltpu.VMEM(activations.shape, BF16),
             pltpu.VMEM((layers, channels, 2 * height * frames * width), BF16),
             pltpu.VMEM((layers, 2, height + 2, frames, width, rank), BF16),
@@ -313,7 +366,6 @@
             pltpu.VMEM((chunks,) + blocks, BF16),
             pltpu.VMEM((chunks, 2) + blocks, BF16),
             pltpu.VMEM((chunks, 2) + blocks, BF16),
-            pltpu.VMEM((8, 128), F32),
             pltpu.VMEM((layers,) + blocks, STAGE2),
             pltpu.VMEM((layers,) + blocks, STAGE2),
             pltpu.VMEM((layers, 2) + blocks, STAGE2),
@@ -321,11 +373,14 @@
             pltpu.VMEM((layers,) + blocks, F32),
             pltpu.VMEM((layers, 3, WIN, rank), F32),
             pltpu.VMEM((layers, rank, rank), F32),
-            pltpu.VMEM((4, layers, rank // 2, rank), F32),
-            pltpu.VMEM((layers, rank // 2, rank), F32),
-            pltpu.VMEM((3, 3, layers, rank // 2, rank), F32),
+            pltpu.VMEM((rank, rank), F32),
+            pltpu.VMEM((2, rank, rank), F32),
+            pltpu.VMEM((3, rank // RING, rank), F32),
+            pltpu.VMEM((3, rank // RING, rank), F32),
+            pltpu.VMEM((2, 3, rank // RING, rank), F32),
             pltpu.SemaphoreType.DMA((80,)),
             pltpu.SemaphoreType.DMA((80,)),
+            pltpu.SemaphoreType.DMA((2 * layers,)),
         ],
         compiler_params=pltpu.CompilerParams(
             collective_id=0, has_side_effects=True, vmem_limit_bytes=60 * 2**20

time: 95.2 us -> 87.5 us (0.919)
  Pallas kernels: 93.4 us -> 85.6 us
    pallas_call x1, Pallas kernels: 83.9 us -> 76.2 us  [shards(): pl.pallas_call(reduce_kernel, name='reduce', out_shape=(jax.ShapeDtypeStr...]
where the time goes in v2:
time: 87.5 us; the launch traced here: 87.3 us
  Pallas kernels  85.6 us (98%)
  local copies, waits for them, and re-layouts  1.67 us (2%)
    pallas_call x1, Pallas kernels, shards(): pl.pallas_call(reduce_kernel, name='reduce', out_shape=(jax.ShapeDtypeStr...  76.2 us
    pallas_call x1, Pallas kernels, shards(): pl.pallas_call(functools.partial(factor_kernel, scale=math.sqrt(27 * chan...  9.45 us

profile of v2, /device:TPU:1, one launch (start us, length us, event | category | flops | bytes accessed | tf_op | source)
XLA Modules:
  0.0 87.3 jit_solution(4197765788281630693)
XLA Ops:
  0.0 76.2 %reduce.1 = (f32[2,176,128]{2,1,0:T(8,128)}, f32[2,128,128]{2,1,0:T(8,128)}) custom-call(bf16[2,1,8,2,32,768]{5,4,3,2,1,0:T(8,128)(2,1)} %act_in.1, bf16[2,1,8,2,32,768]{5,4,3,2,1,0:T(8,128)(2,1)} %grads_in.1, bf16[768,128]{1,0:T(8,128)(2,1)} %omega.1), custom_call_target="tpu_custom_call" | custom-call | tf_op jit(solution)/shard_map/reduce/pallas_call | solution.py:348
  76.2 9.5 %factor.1 = f32[2,162,128]{2,1,0:T(8,128)} custom-call(f32[2,176,128]{2,1,0:T(8,128)} %get-tuple-element.7.rows, f32[2,128,128]{2,1,0:T(8,128)} %get-tuple-element.8.gram), custom_call_target="tpu_custom_call" | custom-call | tf_op jit(solution)/shard_map/factor/pallas_call | solution.py:389
  85.6 1.7 %copy.4 = f32[2,162,128]{2,0,1:T(2,128)} copy(f32[2,162,128]{2,1,0:T(8,128)} %factor.1) | data formatting | bytes 331776 | tf_op jit(solution)/shard_map/factor/pallas_call | solution.py:389

commit v3 on v2

--- a/solution.py
+++ b/solution.py
@@ -18,7 +18,7 @@
 SLAB = 6
 ORDER = (2, 1, 3, 0)
 CHUNKS = [(r, l) for r in ORDER for l in (0, 1)]
-PANEL = 8
+PANEL = 16
 LAG2, LAG3 = 2, 4
 STAGE2 = BF16
 
@@ -27,7 +27,7 @@
     act_in, grads_in, omega, rows_out, gram_out,
     act, grads, act2, act_t, sk, ext, slab, send1, recv1, send2, recv2,
     send3, recv3, send4, recv4, part2, recv5,
-    gram, recv6, full, recv7, quarter, recv8, ssem, rsem, lsem,
+    gram, recv6, part, recv7, ssem, rsem, lsem,
 ):
     layers, _, frames, height, width, channels = act_in.shape
     rank = omega.shape[1]
@@ -47,7 +47,15 @@
     spaces = RING * RING
     below, above = (space + 1) % spaces, (space + spaces - 1) % spaces
     halo = [{"dp": dp, "space": at} for at in (below, above)]
-    peers = [partner] + halo + [along(a, j) for a in ("x", "y", "z") for j in (1, 2, 3)]
+    turns = [(a, b) for a in range(RING) for b in range(RING) if a or b]
+    plane = [
+        {"dp": dp, "space": (x + a) % RING * RING + (z + b) % RING} for a, b in turns
+    ]
+    column_turns = [(a, c) for a in range(RING) for c in range(2) if a or c]
+    stack = [
+        {"dp": (y + a) % RING * 2 + (core + c) % 2, "space": space} for a, c in column_turns
+    ]
+    peers = plane + stack
 
     barrier = pltpu.get_barrier_semaphore()
     for peer in peers:
@@ -264,34 +272,28 @@
         value = pltpu.roll(value, (WIN - shift) % WIN, 0)
         value = jnp.where(row < OWN, value, 0.0)
         rows_out[l] = value
-        gram[l] = lax.dot_general(
+        product = lax.dot_general(
             value, value, (((0,), (0,)), ((), ())), precision=HIGHEST, preferred_element_type=F32
         )
-
-    copy = send(gram.at[1 - core], recv6, partner)
-    copy.wait_recv()
-    full[0] = gram[core] + recv6[...]
-    part = rank // RING
-
-    def rows_of(step):
-        return pl.ds(pl.multiple_of((y + step) % RING * part, part), part)
-
-    copies = [send(full.at[0, rows_of(j)], recv7.at[j - 1], along("y", j)) for j in (1, 2, 3)]
+        gram[l * rank // 16:(l + 1) * rank // 16] = product.reshape(rank // 16, 16, rank)
+
+    copies = [
+        send(gram.at[to["space"]], recv6.at[n], to) for n, to in enumerate(plane)
+    ]
+    value = gram[space]
+    for n, copy in enumerate(copies):
+        copy.wait_recv()
+        value = value + recv6[n]
+    part[0] = value
+    copies = [send(part.at[0], recv7.at[n], to) for n, to in enumerate(stack)]
+    for n, copy in enumerate(copies):
+        copy.wait_recv()
+        value = value + recv7[n]
+    part[1] = value
+    gram_out[space] = value
+    copies = [send(part.at[1], gram_out.at[space], to) for to in plane]
     for copy in copies:
         copy.wait_recv()
-    quarter[0] = full[0, rows_of(0)] + recv7[0] + recv7[1] + recv7[2]
-    for s, axis in enumerate(("x", "z")):
-        copies = [send(quarter.at[s], recv8.at[s, j - 1], along(axis, j)) for j in (1, 2, 3)]
-        for copy in copies:
-            copy.wait_recv()
-        quarter[s + 1] = quarter[s] + recv8[s, 0] + recv8[s, 1] + recv8[s, 2]
-    copies = [send(quarter.at[2], full.at[1, rows_of(0)], along("y", j)) for j in (1, 2, 3)]
-    full[1, rows_of(0)] = quarter[2]
-    for copy in copies:
-        copy.wait_recv()
-    copy = send(full.at[1], gram_out.at[core], partner)
-    gram_out[core] = full[1]
-    copy.wait_recv()
     for copy in sent:
         copy.wait_send()
 
@@ -304,39 +306,47 @@
     work[...] = gram[...]
     for p in range(rank // PANEL):
         first = p * PANEL
+        rest = first + PANEL
+        at = lane - first
         for l in range(layers):
-            panel = work[l, first:first + PANEL]
+            lower = work[l, first:rest]
+            solved = lower
             cols = [
-                jnp.broadcast_to(panel[:, first + j:first + j + 1], (PANEL, rank)) for j in range(PANEL)
+                jnp.broadcast_to(lower[:, first + j:first + j + 1], (PANEL, rank)) for j in range(PANEL)
             ]
-            pivots = jnp.ones((PANEL, rank), F32)
+            roots = jnp.ones((PANEL, rank), F32)
             for j in range(PANEL):
+                own = row == j
                 pivot = jnp.broadcast_to(cols[j][j:j + 1], (PANEL, rank))
-                pivots = jnp.where(row == j, pivot, pivots)
-                if j < PANEL - 1:
-                    mult = jnp.where(row > j, cols[j] / pivot, 0.0)
-                    updated = panel - mult * panel[j:j + 1]
-                    panel = jnp.where((lane == first + j) & (row > j), -mult, updated)
-                    for i in range(j + 1, PANEL):
-                        cols[i] = cols[i] - mult * cols[i][j:j + 1]
-            inside = (lane >= first) & (lane < first + PANEL)
-            unit = jnp.where(lane - first < row, panel, jnp.where(lane - first == row, 1.0, 0.0))
-            full = jnp.where(inside, unit, panel)
-            inverse[l, first:first + PANEL] = jnp.where(lane - first <= row, full, 0.0) / jnp.sqrt(pivots)
-            if first + PANEL < rank:
-                step = lax.dot_general(
-                    panel / pivots, full, (((0,), (0,)), ((), ())),
-                    precision=HIGHEST, preferred_element_type=F32,
+                roots = jnp.where(own, pivot, roots)
+                scaled = 1.0 / pivot
+                mult = cols[j] * scaled
+                for i in range(j + 1, PANEL):
+                    line = jnp.broadcast_to(cols[i][j:j + 1], (PANEL, rank))
+                    cols[i] = jnp.where(own, line * scaled, cols[i] - mult * line)
+                line = jnp.broadcast_to(solved[j:j + 1], (PANEL, rank))
+                pick = jnp.where(own, scaled, -mult)
+                solved = jnp.where(at == j, pick, jnp.where(own, line * scaled, solved - mult * line))
+                below = jnp.where(row > j, mult, 0.0)
+                updated = lower - below * lower[j:j + 1]
+                lower = jnp.where((at == j) & (row > j), -mult, updated)
+            lower = jnp.where(at < row, lower, jnp.where(at == row, 1.0, 0.0))
+            inverse[l, first:rest] = lower / jnp.sqrt(roots)
+            if rest < rank:
+                parts = [jnp.zeros((first, rank), F32)] if first else []
+                parts += [solved, jnp.zeros((rank - rest, rank), F32)]
+                left = work[l, rest:]
+                step = jnp.dot(
+                    left, jnp.concatenate(parts, axis=0), precision=HIGHEST, preferred_element_type=F32
                 )
-                rest = first + PANEL
-                in_wide = (wide[rest:] >= first) & (wide[rest:] < rest)
-                work[l, rest:] = jnp.where(in_wide, 0.0, work[l, rest:]) - step[rest:]
+                inside = (wide[rest:] >= first) & (wide[rest:] < rest)
+                work[l, rest:] = jnp.where(inside, 0.0, left) - step
     for l in range(layers):
         value = lax.dot_general(
             rows[l], inverse[l], (((1,), (1,)), ((), ())),
             precision=HIGHEST, preferred_element_type=F32,
         )
-        out[l] = (value * scale)[:OWN]
+        out[:, l] = (value * scale)[:OWN]
 
 
 def shards(activations, out_grads, omega):
@@ -350,7 +360,7 @@
         name="reduce",
         out_shape=(
             jax.ShapeDtypeStruct((layers, WIN, rank), F32),
-            jax.ShapeDtypeStruct((layers, rank, rank), F32),
+            jax.ShapeDtypeStruct((RING * RING, 16, rank), F32),
         ),
         in_specs=[pl.BlockSpec(memory_space=pl.ANY)] * 2 + [vmem],
         out_specs=(vmem, vmem),
@@ -372,31 +382,30 @@
             pltpu.VMEM((layers, 2) + blocks, STAGE2),
             pltpu.VMEM((layers,) + blocks, F32),
             pltpu.VMEM((layers, 3, WIN, rank), F32),
-            pltpu.VMEM((layers, rank, rank), F32),
-            pltpu.VMEM((rank, rank), F32),
-            pltpu.VMEM((2, rank, rank), F32),
-            pltpu.VMEM((3, rank // RING, rank), F32),
-            pltpu.VMEM((3, rank // RING, rank), F32),
-            pltpu.VMEM((2, 3, rank // RING, rank), F32),
-            pltpu.SemaphoreType.DMA((80,)),
-            pltpu.SemaphoreType.DMA((80,)),
+            pltpu.VMEM((RING * RING, 16, rank), F32),
+            pltpu.VMEM((RING * RING - 1, 16, rank), F32),
+            pltpu.VMEM((2, 16, rank), F32),
+            pltpu.VMEM((2 * RING - 1, 16, rank), F32),
+            pltpu.SemaphoreType.DMA((112,)),
+            pltpu.SemaphoreType.DMA((112,)),
             pltpu.SemaphoreType.DMA((2 * layers,)),
         ],
         compiler_params=pltpu.CompilerParams(
             collective_id=0, has_side_effects=True, vmem_limit_bytes=60 * 2**20
         ),
     )(activations, out_grads, omega)
-    return pl.pallas_call(
+    basis = pl.pallas_call(
         functools.partial(factor_kernel, scale=math.sqrt(27 * channels)),
         name="factor",
-        out_shape=jax.ShapeDtypeStruct((layers, OWN, rank), F32),
+        out_shape=jax.ShapeDtypeStruct((OWN, layers, rank), F32),
         in_specs=[vmem] * 2,
         out_specs=vmem,
         scratch_shapes=[
             pltpu.VMEM((layers, rank, rank), F32),
             pltpu.VMEM((layers, rank, rank), F32),
         ],
-    )(rows, gram)
+    )(rows, gram.reshape(layers, rank, rank))
+    return jnp.transpose(basis, (1, 0, 2))
 
 
 def solution(mesh):

time: 87.5 us -> 82.6 us (0.944)
  Pallas kernels: 85.6 us -> 82.4 us
  local copies, waits for them, and re-layouts: 1.67 us -> 0 us
    pallas_call x1, Pallas kernels: 9.45 us -> 7.11 us  [shards(): pl.pallas_call(functools.partial(factor_kernel, scale=math.sqrt(27 * chan...]
    pallas_call x1 -> x0, local copies, waits for them, and re-layouts: 1.67 us -> none  [shards(): pl.pallas_call(functools.partial(factor_kernel, scale=math.sqrt(27 * chan...]
    pallas_call x1, Pallas kernels: 76.2 us -> 75.3 us  [shards(): pl.pallas_call(reduce_kernel, name='reduce', out_shape=(jax.ShapeDtypeStr...]
where the time goes in v3:
time: 82.6 us; the launch traced here: 82.4 us
  Pallas kernels  82.4 us (100%)
    pallas_call x1, Pallas kernels, shards(): pl.pallas_call(reduce_kernel, name='reduce', out_shape=(jax.ShapeDtypeStr...  75.3 us
    pallas_call x1, Pallas kernels, shards(): pl.pallas_call(functools.partial(factor_kernel, scale=math.sqrt(27 * chan...  7.11 us

profile of v3, /device:TPU:1, one launch (start us, length us, event | category | flops | bytes accessed | tf_op | source)
XLA Modules:
  0.0 82.4 jit_solution(1550162295367490769)
XLA Ops:
  0.0 75.3 %reduce.1 = (f32[2,176,128]{2,1,0:T(8,128)}, f32[16,16,128]{2,1,0:T(8,128)}) custom-call(bf16[2,1,8,2,32,768]{5,4,3,2,1,0:T(8,128)(2,1)} %act_in.1, bf16[2,1,8,2,32,768]{5,4,3,2,1,0:T(8,128)(2,1)} %grads_in.1, bf16[768,128]{1,0:T(8,128)(2,1)} %omega.1), custom_call_target="tpu_custom_call" | custom-call | tf_op jit(solution)/shard_map/reduce/pallas_call | solution.py:358
  75.3 7.1 %factor.1 = f32[162,2,128]{2,1,0:T(2,128)} custom-call(f32[2,176,128]{2,1,0:T(8,128)} %get-tuple-element.7.rows, f32[2,128,128]{2,1,0:T(8,128)} %bitcast.2), custom_call_target="tpu_custom_call" | custom-call | tf_op jit(solution)/shard_map/factor/pallas_call | solution.py:397

commit v4 on v3

v4 whole, which is shorter than its diff:
```python
import functools
import math

import jax
import jax.numpy as jnp
from jax import lax
from jax.experimental import pallas as pl
from jax.experimental.pallas import tpu as pltpu
from jax.sharding import PartitionSpec as P

MESH = pl.DeviceIdType.MESH
BF16, F32 = jnp.bfloat16, jnp.float32
HIGHEST = lax.Precision.HIGHEST
RING = 4
OWN = 162
WIN = 176
BLOCK = OWN * 16
SLAB = 8
ORDER = (2, 1, 3, 0)
CHUNKS = [(r, e) for r in ORDER for e in (0, 1)]
PANEL = 16
LAG2, LAG3 = 2, 4
STAGE2 = BF16


def reduce_kernel(
    act_in, grads_in, omega, rows_out, gram_out,
    act, grads, act2, act_t, other, sk, ext, slab, send1, recv1, send2, recv2,
    send3, recv3, send4, recv4, part2, recv5, rolled,
    gram, recv6, part, recv7, full, ssem, rsem, lsem,
):
    layers, _, frames, height, width, channels = act_in.shape
    rank = omega.shape[1]
    dp, space = lax.axis_index("dp"), lax.axis_index("space")
    y, core = dp // 2, dp % 2
    x, z = space // RING, space % RING
    other_dp = y * 2 + 1 - core

    def along(axis, step):
        if axis == "x":
            return {"dp": dp, "space": (x + step) % RING * RING + z}
        if axis == "z":
            return {"dp": dp, "space": x * RING + (z + step) % RING}
        return {"dp": (y + step) % RING * 2 + core, "space": space}

    partner = {"dp": other_dp, "space": space}
    spaces = RING * RING
    below, above = (space + 1) % spaces, (space + spaces - 1) % spaces
    turns = [(a, b) for a in range(RING) for b in range(RING) if a or b]
    plane = [
        {"dp": dp, "space": (x + a) % RING * RING + (z + b) % RING} for a, b in turns
    ]
    stack = [along("y", j) for j in (1, 2, 3)]
    crossed = [{"dp": other_dp, "space": below}, {"dp": other_dp, "space": above}]
    peers = [partner] + crossed + plane + stack

    barrier = pltpu.get_barrier_semaphore()
    for peer in peers:
        pl.semaphore_signal(barrier, inc=1, device_id=peer, device_id_type=MESH)

    loads = [
        pltpu.make_async_copy(grads_in.at[1 - core], grads.at[0], lsem.at[0]),
        pltpu.make_async_copy(grads_in.at[core], grads.at[1], lsem.at[1]),
        pltpu.make_async_copy(act_in.at[core], act, lsem.at[2]),
    ]
    for copy in loads:
        copy.start()

    def sketch(n, h):
        flat = grads[n, 0, :, h].reshape(frames * width, channels)
        value = jnp.dot(flat, omega[...], preferred_element_type=F32).astype(BF16)
        return value.reshape(frames, width, rank)

    loads[0].wait()
    for h in range(height):
        other[h] = sketch(0, h)
    loads[1].wait()
    for h in range(height):
        sk[0, 1 + h] = sketch(1, h)

    pl.semaphore_wait(barrier, len(peers))
    sent = []

    def send(src, dst, to):
        at = len(sent)
        copy = pltpu.make_async_remote_copy(
            src_ref=src, dst_ref=dst, send_sem=ssem.at[at], recv_sem=rsem.at[at],
            device_id=to, device_id_type=MESH,
        )
        copy.start()
        sent.append(copy)
        return copy

    halo_copies = [
        [
            send(sk.at[0, height], sk.at[0, 0], {"dp": dp, "space": below}),
            send(sk.at[0, 1], sk.at[0, height + 1], {"dp": dp, "space": above}),
        ],
        [
            send(other.at[height - 1], sk.at[1, 0], crossed[0]),
            send(other.at[0], sk.at[1, height + 1], crossed[1]),
        ],
    ]
    row_copy = send(other, sk.at[1, 1:1 + height], partner)
    act_copy = send(act_in.at[1 - core], act2, partner)

    def transpose(slot, source):
        for h in range(height):
            flat = source[0, :, h].reshape(frames * width, channels)
            at = (slot * height + h) * frames * width
            act_t[:, at:at + frames * width] = flat.T

    column = lax.broadcasted_iota(jnp.int32, (frames * width, rank), 0) % width

    def extend(slot, h):
        value = sk[slot, h].reshape(frames * width, rank).astype(F32)
        if h == 0:
            value = jnp.where(space > 0, value, 0.0)
        if h == height + 1:
            value = jnp.where(space < spaces - 1, value, 0.0)
        ahead = jnp.where(column < width - 1, pltpu.roll(value, frames * width - 1, 0), 0.0)
        behind = jnp.where(column > 0, pltpu.roll(value, 1, 0), 0.0)
        for c, shifted in enumerate((ahead, value, behind)):
            zero = jnp.zeros((width, rank), BF16)
            ext[c, slot, h, 0] = zero
            ext[c, slot, h, frames + 1] = zero
            ext[c, slot, h, 1:1 + frames] = shifted.astype(BF16).reshape(frames, width, rank)

    inner, outer = range(1, 1 + height), (0, height + 1)
    loads[2].wait()
    transpose(0, act)
    for h in inner:
        extend(0, h)
    row_copy.wait_recv()
    for h in inner:
        extend(1, h)
    act_copy.wait_recv()
    transpose(1, act2)
    for slot in range(2):
        for copy, h in zip(halo_copies[slot], outer):
            copy.wait_recv()
            extend(slot, h)

    depth = 2 * height * frames * width

    def compute(r, pairs):
        first = 27 * ((y + r) % RING * 2) // 8

        def columns(k):
            k = jnp.minimum(first + k, 26)
            a, b, c = k // 9, k // 3 % 3, k % 3
            return ext[c, :, pl.ds(2 - b, height), pl.ds(2 - a, frames)].reshape(depth, rank)

        def pair(i, _):
            both = jnp.concatenate([columns(2 * i), columns(2 * i + 1)], axis=1)
            for m in range(3):
                rows = channels // 3
                value = jnp.dot(act_t[m * rows:(m + 1) * rows], both, preferred_element_type=F32)
                for s in range(2):
                    at = pl.multiple_of((2 * i + s) * channels + m * rows, rows)
                    slab[r, pl.ds(at, rows)] = value[:, s * rank:(s + 1) * rank]
            return 0

        lax.fori_loop(pairs[0], pairs[1], pair, 0)

    def window(r, e, mine, o):
        owner = (y + r) % RING * 2 + e
        place = mine * RING + o if e == 0 else o * RING + mine
        start = 27 * owner - 27 * (owner - e) // 8 * 8
        at = start * (channels // 8) + OWN * place // 16 * 16
        return slab[r, pl.ds(pl.multiple_of(at, 16), WIN)]

    first_axis = ("x", "z")
    last_axis = ("z", "x")
    first_at = (x, z)
    last_at = (z, x)
    half1 = RING // 2
    step1, step2, step3, step4, step5 = {}, {}, {}, {}, {}

    def start1(n):
        r, e = CHUNKS[n]
        for o in range(RING):
            send1[n, o] = window(r, e, (first_at[e] + 2) % RING, o).astype(BF16)
        step1[n] = [
            send(send1.at[n, :half1], recv1.at[n, :half1], along(first_axis[e], 1)),
            send(send1.at[n, half1:], recv1.at[n, half1:], along(first_axis[e], 3)),
        ]

    def start2(n):
        r, e = CHUNKS[n]
        copies = []
        for s, step in enumerate((1, 3)):
            step1[n][s].wait_recv()
            for o in range(RING):
                value = window(r, e, (first_at[e] + step) % RING, o)
                if (o < half1) == (s == 0):
                    value = value + recv1[n, o].astype(F32)
                send2[n, s, o] = value.astype(BF16)
            copies.append(send(send2.at[n, s], recv2.at[n, s], along(first_axis[e], step)))
        step2[n] = copies

    def finish1(n):
        r, e = CHUNKS[n]
        for copy in step2[n]:
            copy.wait_recv()
        if r in (1, 3):
            step3[e][0 if r == 1 else 1].wait_recv()
        if r == 0:
            for copy in step4[e]:
                copy.wait_recv()
        for o in range(RING):
            value = window(r, e, first_at[e], o)
            value = value + recv2[n, 0, o].astype(F32) + recv2[n, 1, o].astype(F32)
            if r == 2:
                send3[e, o] = value.astype(STAGE2)
            elif r == 0:
                part2[e, o] = value + recv4[e, 0, o].astype(F32) + recv4[e, 1, o].astype(F32)
            else:
                s = 0 if r == 1 else 1
                if (o < half1) == (s == 0):
                    value = value + recv3[e, o].astype(F32)
                send4[e, s, o] = value.astype(STAGE2)
        if r == 2:
            step3[e] = [
                send(send3.at[e, :half1], recv3.at[e, :half1], along("y", 1)),
                send(send3.at[e, half1:], recv3.at[e, half1:], along("y", 3)),
            ]
        elif r == 0:
            step5[e] = [
                send(part2.at[e, (last_at[e] + j) % RING], recv5.at[e, j - 1], along(last_axis[e], j))
                for j in (1, 2, 3)
            ]
        else:
            s = 0 if r == 1 else 1
            step4.setdefault(e, []).append(send(send4.at[e, s], recv4.at[e, s], along("y", r)))

    total = len(CHUNKS)
    for n in range(total + LAG3):
        if n < total:
            r, e = CHUNKS[n]
            compute(r, ((0, 3), (3, 4))[e])
            start1(n)
        if LAG2 <= n < total + LAG2:
            start2(n - LAG2)
        if n >= LAG3:
            finish1(n - LAG3)

    shift = 2 * space % 16
    row = lax.broadcasted_iota(jnp.int32, (WIN, rank), 0)
    product = jnp.zeros((rank, rank), F32)
    for e in range(2):
        for copy in step5[e]:
            copy.wait_recv()
        value = part2[e, last_at[e]] + recv5[e, 0] + recv5[e, 1] + recv5[e, 2]
        value = pltpu.roll(value, (WIN - shift) % WIN, 0)
        value = jnp.where(row < OWN, value, 0.0)
        rolled[e] = value
        product = product + lax.dot_general(
            value, value, (((0,), (0,)), ((), ())), precision=HIGHEST, preferred_element_type=F32
        )
    gram[...] = product.reshape(spaces, rank // spaces, rank)

    copies = [send(gram.at[to["space"]], recv6.at[n], to) for n, to in enumerate(plane)]
    rows_copy = send(rolled.at[1 - core], rows_out.at[core], partner)
    rows_out[core] = rolled[core]
    value = gram[space]
    for n, copy in enumerate(copies):
        copy.wait_recv()
        value = value + recv6[n]
    part[0] = value
    copies = [send(part.at[0], recv7.at[n], to) for n, to in enumerate(stack)]
    for n, copy in enumerate(copies):
        copy.wait_recv()
        value = value + recv7[n]
    part[1] = value
    full[space] = value
    copies = [send(part.at[1], full.at[space], to) for to in plane]
    for copy in copies:
        copy.wait_recv()
    copy = send(full, gram_out.at[core], partner)
    gram_out[core] = full[...]
    copy.wait_recv()
    rows_copy.wait_recv()
    for copy in sent:
        copy.wait_send()


def factor_kernel(rows, gram, out, work, inverse, *, scale):
    layers, rank, _ = gram.shape
    lane = lax.broadcasted_iota(jnp.int32, (PANEL, rank), 1)
    row = lax.broadcasted_iota(jnp.int32, (PANEL, rank), 0)
    wide = lax.broadcasted_iota(jnp.int32, (rank, rank), 1)
    work[...] = gram[...]
    for p in range(rank // PANEL):
        first = p * PANEL
        rest = first + PANEL
        at = lane - first
        for l in range(layers):
            lower = work[l, first:rest]
            solved = lower
            cols = [
                jnp.broadcast_to(lower[:, first + j:first + j + 1], (PANEL, rank)) for j in range(PANEL)
            ]
            roots = jnp.ones((PANEL, rank), F32)
            for j in range(PANEL):
                own = row == j
                pivot = jnp.broadcast_to(cols[j][j:j + 1], (PANEL, rank))
                roots = jnp.where(own, pivot, roots)
                scaled = 1.0 / pivot
                mult = cols[j] * scaled
                for i in range(j + 1, PANEL):
                    line = jnp.broadcast_to(cols[i][j:j + 1], (PANEL, rank))
                    cols[i] = jnp.where(own, line * scaled, cols[i] - mult * line)
                line = jnp.broadcast_to(solved[j:j + 1], (PANEL, rank))
                pick = jnp.where(own, scaled, -mult)
                solved = jnp.where(at == j, pick, jnp.where(own, line * scaled, solved - mult * line))
                below = jnp.where(row > j, mult, 0.0)
                updated = lower - below * lower[j:j + 1]
                lower = jnp.where((at == j) & (row > j), -mult, updated)
            lower = jnp.where(at < row, lower, jnp.where(at == row, 1.0, 0.0))
            inverse[l, first:rest] = lower / jnp.sqrt(roots)
            if rest < rank:
                parts = [jnp.zeros((first, rank), F32)] if first else []
                parts += [solved, jnp.zeros((rank - rest, rank), F32)]
                left = work[l, rest:]
                step = jnp.dot(
                    left, jnp.concatenate(parts, axis=0), precision=HIGHEST, preferred_element_type=F32
                )
                inside = (wide[rest:] >= first) & (wide[rest:] < rest)
                work[l, rest:] = jnp.where(inside, 0.0, left) - step
    for l in range(layers):
        value = lax.dot_general(
            rows[l], inverse[l], (((1,), (1,)), ((), ())),
            precision=HIGHEST, preferred_element_type=F32,
        )
        out[:, l] = (value * scale)[:OWN]


def shards(activations, out_grads, omega):
    layers, clips, frames, height, width, channels = activations.shape
    rank = omega.shape[1]
    chunks = len(CHUNKS)
    vmem = pl.BlockSpec(memory_space=pltpu.VMEM)
    blocks = (RING, WIN, rank)
    gram_blocks = (RING * RING, rank // (RING * RING), rank)
    rows, gram = pl.pallas_call(
        reduce_kernel,
        name="reduce",
        out_shape=(
            jax.ShapeDtypeStruct((layers, WIN, rank), F32),
            jax.ShapeDtypeStruct((layers,) + gram_blocks, F32),
        ),
        in_specs=[pl.BlockSpec(memory_space=pl.ANY)] * 2 + [vmem],
        out_specs=(vmem, vmem),
        scratch_shapes=[
            pltpu.VMEM(activations.shape[1:], BF16),
            pltpu.VMEM(activations.shape, BF16),
            pltpu.VMEM(activations.shape[1:], BF16),
            pltpu.VMEM((channels, 2 * height * frames * width), BF16),
            pltpu.VMEM((height, frames, width, rank), BF16),
            pltpu.VMEM((2, height + 2, frames, width, rank), BF16),
            pltpu.VMEM((3, 2, height + 2, frames + 2, width, rank), BF16),
            pltpu.VMEM((RING, SLAB * channels, rank), F32),
            pltpu.VMEM((chunks,) + blocks, BF16),
            pltpu.VMEM((chunks,) + blocks, BF16),
            pltpu.VMEM((chunks, 2) + blocks, BF16),
            pltpu.VMEM((chunks, 2) + blocks, BF16),
            pltpu.VMEM((2,) + blocks, STAGE2),
            pltpu.VMEM((2,) + blocks, STAGE2),
            pltpu.VMEM((2, 2) + blocks, STAGE2),
            pltpu.VMEM((2, 2) + blocks, STAGE2),
            pltpu.VMEM((2,) + blocks, F32),
            pltpu.VMEM((2, 3, WIN, rank), F32),
            pltpu.VMEM((2, WIN, rank), F32),
            pltpu.VMEM(gram_blocks, F32),
            pltpu.VMEM((RING * RING - 1,) + gram_blocks[1:], F32),
            pltpu.VMEM((2,) + gram_blocks[1:], F32),
            pltpu.VMEM((RING - 1,) + gram_blocks[1:], F32),
            pltpu.VMEM(gram_blocks, F32),
            pltpu.SemaphoreType.DMA((112,)),
            pltpu.SemaphoreType.DMA((112,)),
            pltpu.SemaphoreType.DMA((3,)),
        ],
        compiler_params=pltpu.CompilerParams(
            collective_id=0, has_side_effects=True, vmem_limit_bytes=60 * 2**20
        ),
    )(activations, out_grads, omega)
    basis = pl.pallas_call(
        functools.partial(factor_kernel, scale=math.sqrt(27 * channels)),
        name="factor",
        out_shape=jax.ShapeDtypeStruct((OWN, layers, rank), F32),
        in_specs=[vmem] * 2,
        out_specs=vmem,
        scratch_shapes=[
            pltpu.VMEM((layers, rank, rank), F32),
            pltpu.VMEM((layers, rank, rank), F32),
        ],
    )(rows, gram.reshape(layers, rank, rank))
    return jnp.transpose(basis, (1, 0, 2))


def solution(mesh):
    return jax.shard_map(
        shards,
        mesh=mesh,
        in_specs=(
            P(None, "dp", None, "space", None, None),
            P(None, "dp", None, "space", None, None),
            P(),
        ),
        out_specs=P(None, ("dp", "space"), None),
        check_vma=False,
    )
```

time: 82.6 us -> 79.3 us (0.960)
  Pallas kernels: 82.4 us -> 79.2 us
    pallas_call x1, Pallas kernels: 75.3 us -> 72 us  [shards(): pl.pallas_call(reduce_kernel, name='reduce', out_shape=(jax.ShapeDtypeStr...]
where the time goes in v4:
time: 79.3 us; the launch traced here: 79.2 us
  Pallas kernels  79.2 us (100%)
    pallas_call x1, Pallas kernels, shards(): pl.pallas_call(reduce_kernel, name='reduce', out_shape=(jax.ShapeDtypeStr...  72 us
    pallas_call x1, Pallas kernels, shards(): pl.pallas_call(functools.partial(factor_kernel, scale=math.sqrt(27 * chan...  7.12 us

profile of v4, /device:TPU:1, one launch (start us, length us, event | category | flops | bytes accessed | tf_op | source)
XLA Modules:
  0.0 79.2 jit_solution(5892246173007395627)
XLA Ops:
  0.0 72.0 %reduce.1 = (f32[2,176,128]{2,1,0:T(8,128)}, f32[2,16,8,128]{3,2,1,0:T(8,128)}) custom-call(bf16[2,1,8,2,32,768]{5,4,3,2,1,0:T(8,128)(2,1)} %act_in.1, bf16[2,1,8,2,32,768]{5,4,3,2,1,0:T(8,128)(2,1)} %grads_in.1, bf16[768,128]{1,0:T(8,128)(2,1)} %omega.1), custom_call_target="tpu_custom_call" | custom-call | tf_op jit(solution)/shard_map/reduce/pallas_call | solution.py:346
  72.0 7.1 %factor.1 = f32[162,2,128]{2,1,0:T(2,128)} custom-call(f32[2,176,128]{2,1,0:T(8,128)} %get-tuple-element.7.rows, f32[2,128,128]{2,1,0:T(8,128)} %bitcast.2), custom_call_target="tpu_custom_call" | custom-call | tf_op jit(solution)/shard_map/factor/pallas_call | solution.py:388

commit v5 on v4

--- a/solution.py
+++ b/solution.py
@@ -19,14 +19,20 @@
 ORDER = (2, 1, 3, 0)
 CHUNKS = [(r, e) for r in ORDER for e in (0, 1)]
 PANEL = 16
-LAG2, LAG3 = 2, 4
+SCHEDULE = (
+    "C0", "S0", "C1", "S1", "T0", "T1", "C2", "S2", "C3", "S3", "M0", "P1", "P0", "M1", "C4", "S4",
+    "T2", "T4", "M2", "P2", "C5", "S5", "P3", "C6", "F1", "M3", "F0", "P4", "M4", "C7", "S7", "T5",
+    "M5", "P5", "S6", "T6", "T3", "F2", "F4", "M7", "P7", "M6", "F3", "P6", "T7", "F5", "F6", "Z0",
+    "F7", "Z1",
+)
 STAGE2 = BF16
 
 
 def reduce_kernel(
     act_in, grads_in, omega, rows_out, gram_out,
     act, grads, act2, act_t, other, sk, ext, slab, send1, recv1, send2, recv2,
-    send3, recv3, send4, recv4, part2, recv5, rolled,
+    send3, recv3, send4, recv4, send6, recv9, send8, recv8, send9, recv10, mine,
+    part2, recv5, rolled,
     gram, recv6, part, recv7, full, ssem, rsem, lsem,
 ):
     layers, _, frames, height, width, channels = act_in.shape
@@ -174,33 +180,40 @@
     last_axis = ("z", "x")
     first_at = (x, z)
     last_at = (z, x)
-    half1 = RING // 2
+    half = RING // 2
     step1, step2, step3, step4, step5 = {}, {}, {}, {}, {}
+    turn1, turn2, turn3 = {}, {}, {}
+
+    def add(pieces):
+        return functools.reduce(lambda a, b: a + b.astype(F32), pieces)
 
     def start1(n):
         r, e = CHUNKS[n]
-        for o in range(RING):
-            send1[n, o] = window(r, e, (first_at[e] + 2) % RING, o).astype(BF16)
+        cut = 1 + n // 2 % 2
+        for o in range(1, RING):
+            send1[n, o - 1] = window(r, e, (first_at[e] + 2) % RING, o).astype(BF16)
         step1[n] = [
-            send(send1.at[n, :half1], recv1.at[n, :half1], along(first_axis[e], 1)),
-            send(send1.at[n, half1:], recv1.at[n, half1:], along(first_axis[e], 3)),
+            send(send1.at[n, :cut], recv1.at[n, :cut], along(first_axis[e], 1)),
+            send(send1.at[n, cut:], recv1.at[n, cut:], along(first_axis[e], 3)),
         ]
 
-    def start2(n):
+    def start2(n, s):
         r, e = CHUNKS[n]
-        copies = []
-        for s, step in enumerate((1, 3)):
-            step1[n][s].wait_recv()
-            for o in range(RING):
-                value = window(r, e, (first_at[e] + step) % RING, o)
-                if (o < half1) == (s == 0):
-                    value = value + recv1[n, o].astype(F32)
-                send2[n, s, o] = value.astype(BF16)
-            copies.append(send(send2.at[n, s], recv2.at[n, s], along(first_axis[e], step)))
-        step2[n] = copies
+        cut = 1 + n // 2 % 2
+        step = 1 + 2 * s
+        step1[n][s].wait_recv()
+        for o in range(1, RING):
+            value = window(r, e, (first_at[e] + step) % RING, o)
+            if (o <= cut) == (s == 0):
+                value = add([value, recv1[n, o - 1]])
+            send2[n, s, o - 1] = value.astype(BF16)
+        step2.setdefault(n, []).append(
+            send(send2.at[n, s], recv2.at[n, s], along(first_axis[e], step))
+        )
 
     def finish1(n):
         r, e = CHUNKS[n]
+        cut = 1 + e
         for copy in step2[n]:
             copy.wait_recv()
         if r in (1, 3):
@@ -208,42 +221,78 @@
         if r == 0:
             for copy in step4[e]:
                 copy.wait_recv()
-        for o in range(RING):
-            value = window(r, e, first_at[e], o)
-            value = value + recv2[n, 0, o].astype(F32) + recv2[n, 1, o].astype(F32)
+        for o in range(1, RING):
+            p = o - 1
+            value = add([window(r, e, first_at[e], o), recv2[n, 0, p], recv2[n, 1, p]])
             if r == 2:
-                send3[e, o] = value.astype(STAGE2)
+                send3[e, p] = value.astype(STAGE2)
             elif r == 0:
-                part2[e, o] = value + recv4[e, 0, o].astype(F32) + recv4[e, 1, o].astype(F32)
+                part2[e, o] = add([value, recv4[e, 0, p], recv4[e, 1, p]])
             else:
                 s = 0 if r == 1 else 1
-                if (o < half1) == (s == 0):
-                    value = value + recv3[e, o].astype(F32)
-                send4[e, s, o] = value.astype(STAGE2)
+                if (o <= cut) == (s == 0):
+                    value = add([value, recv3[e, p]])
+                send4[e, s, p] = value.astype(STAGE2)
         if r == 2:
             step3[e] = [
-                send(send3.at[e, :half1], recv3.at[e, :half1], along("y", 1)),
-                send(send3.at[e, half1:], recv3.at[e, half1:], along("y", 3)),
+                send(send3.at[e, :cut], recv3.at[e, :cut], along("y", 1)),
+                send(send3.at[e, cut:], recv3.at[e, cut:], along("y", 3)),
+            ]
+        elif r in (1, 3):
+            s = 0 if r == 1 else 1
+            step4.setdefault(e, []).append(send(send4.at[e, s], recv4.at[e, s], along("y", r)))
+
+    def turn(n):
+        r, e = CHUNKS[n]
+        s = 0 if r == 1 else 1
+        if r in (1, 3):
+            turn1[e][s].wait_recv()
+        if r == 0:
+            for copy in turn2[e]:
+                copy.wait_recv()
+        for a in range(RING):
+            value = window(r, e, a, 0)
+            if r == 2:
+                send6[e, a] = value.astype(BF16)
+            elif r == 0:
+                value = add([value, recv8[e, 0, a], recv8[e, 1, a]])
+                send9[e, a] = value.astype(STAGE2)
+                mine[e, a] = value
+            else:
+                if (a < half) == (s == 0):
+                    value = add([value, recv9[e, a]])
+                send8[e, s, a] = value.astype(BF16)
+        if r == 2:
+            turn1[e] = [
+                send(send6.at[e, :half], recv9.at[e, :half], along("y", 1)),
+                send(send6.at[e, half:], recv9.at[e, half:], along("y", 3)),
             ]
         elif r == 0:
-            step5[e] = [
-                send(part2.at[e, (last_at[e] + j) % RING], recv5.at[e, j - 1], along(last_axis[e], j))
+            turn3[e] = [
+                send(send9.at[e, (first_at[e] + j) % RING], recv10.at[e, j - 1], along(first_axis[e], j))
                 for j in (1, 2, 3)
             ]
         else:
-            s = 0 if r == 1 else 1
-            step4.setdefault(e, []).append(send(send4.at[e, s], recv4.at[e, s], along("y", r)))
-
-    total = len(CHUNKS)
-    for n in range(total + LAG3):
-        if n < total:
+            turn2.setdefault(e, []).append(send(send8.at[e, s], recv8.at[e, s], along("y", r)))
+
+    def finish2(e):
+        for copy in turn3[e]:
+            copy.wait_recv()
+        part2[e, 0] = add([mine[e, first_at[e]], recv10[e, 0], recv10[e, 1], recv10[e, 2]])
+        step5[e] = [
+            send(part2.at[e, (last_at[e] + j) % RING], recv5.at[e, j - 1], along(last_axis[e], j))
+            for j in (1, 2, 3)
+        ]
+
+    for entry in SCHEDULE:
+        n = int(entry[1:])
+        if entry[0] == "C":
             r, e = CHUNKS[n]
             compute(r, ((0, 3), (3, 4))[e])
-            start1(n)
-        if LAG2 <= n < total + LAG2:
-            start2(n - LAG2)
-        if n >= LAG3:
-            finish1(n - LAG3)
+        elif entry[0] in "PM":
+            start2(n, "PM".index(entry[0]))
+        else:
+            {"S": start1, "T": turn, "F": finish1, "Z": finish2}[entry[0]](n)
 
     shift = 2 * space % 16
     row = lax.broadcasted_iota(jnp.int32, (WIN, rank), 0)
@@ -341,7 +390,7 @@
     rank = omega.shape[1]
     chunks = len(CHUNKS)
     vmem = pl.BlockSpec(memory_space=pltpu.VMEM)
-    blocks = (RING, WIN, rank)
+    blocks, fewer = (RING, WIN, rank), (RING - 1, WIN, rank)
     gram_blocks = (RING * RING, rank // (RING * RING), rank)
     rows, gram = pl.pallas_call(
         reduce_kernel,
@@ -361,14 +410,21 @@
             pltpu.VMEM((2, height + 2, frames, width, rank), BF16),
             pltpu.VMEM((3, 2, height + 2, frames + 2, width, rank), BF16),
             pltpu.VMEM((RING, SLAB * channels, rank), F32),
-            pltpu.VMEM((chunks,) + blocks, BF16),
-            pltpu.VMEM((chunks,) + blocks, BF16),
-            pltpu.VMEM((chunks, 2) + blocks, BF16),
-            pltpu.VMEM((chunks, 2) + blocks, BF16),
+            pltpu.VMEM((chunks,) + fewer, BF16),
+            pltpu.VMEM((chunks,) + fewer, BF16),
+            pltpu.VMEM((chunks, 2) + fewer, BF16),
+            pltpu.VMEM((chunks, 2) + fewer, BF16),
+            pltpu.VMEM((2,) + fewer, STAGE2),
+            pltpu.VMEM((2,) + fewer, STAGE2),
+            pltpu.VMEM((2, 2) + fewer, STAGE2),
+            pltpu.VMEM((2, 2) + fewer, STAGE2),
+            pltpu.VMEM((2,) + blocks, BF16),
+            pltpu.VMEM((2,) + blocks, BF16),
+            pltpu.VMEM((2, 2) + blocks, BF16),
+            pltpu.VMEM((2, 2) + blocks, BF16),
             pltpu.VMEM((2,) + blocks, STAGE2),
-            pltpu.VMEM((2,) + blocks, STAGE2),
-            pltpu.VMEM((2, 2) + blocks, STAGE2),
-            pltpu.VMEM((2, 2) + blocks, STAGE2),
+            pltpu.VMEM((2,) + fewer, STAGE2),
+            pltpu.VMEM((2,) + blocks, F32),
             pltpu.VMEM((2,) + blocks, F32),
             pltpu.VMEM((2, 3, WIN, rank), F32),
             pltpu.VMEM((2, WIN, rank), F32),

time: 79.3 us -> 74.1 us (0.934)
  Pallas kernels: 79.2 us -> 74 us
    pallas_call x1, Pallas kernels: 72 us -> 66.9 us  [shards(): pl.pallas_call(reduce_kernel, name='reduce', out_shape=(jax.ShapeDtypeStr...]
where the time goes in v5:
time: 74.1 us; the launch traced here: 74 us
  Pallas kernels  74 us (100%)
    pallas_call x1, Pallas kernels, shards(): pl.pallas_call(reduce_kernel, name='reduce', out_shape=(jax.ShapeDtypeStr...  66.9 us
    pallas_call x1, Pallas kernels, shards(): pl.pallas_call(functools.partial(factor_kernel, scale=math.sqrt(27 * chan...  7.11 us

profile of v5, /device:TPU:1, one launch (start us, length us, event | category | flops | bytes accessed | tf_op | source)
XLA Modules:
  0.0 74.0 jit_solution(15371101223378511005)
XLA Ops:
  0.0 66.9 %reduce.1 = (f32[2,176,128]{2,1,0:T(8,128)}, f32[2,16,8,128]{3,2,1,0:T(8,128)}) custom-call(bf16[2,1,8,2,32,768]{5,4,3,2,1,0:T(8,128)(2,1)} %act_in.1, bf16[2,1,8,2,32,768]{5,4,3,2,1,0:T(8,128)(2,1)} %grads_in.1, bf16[768,128]{1,0:T(8,128)(2,1)} %omega.1), custom_call_target="tpu_custom_call" | custom-call | tf_op jit(solution)/shard_map/reduce/pallas_call | solution.py:395
  66.9 7.1 %factor.1 = f32[162,2,128]{2,1,0:T(2,128)} custom-call(f32[2,176,128]{2,1,0:T(8,128)} %get-tuple-element.7.rows, f32[2,128,128]{2,1,0:T(8,128)} %bitcast.2), custom_call_target="tpu_custom_call" | custom-call | tf_op jit(solution)/shard_map/factor/pallas_call | solution.py:444

commit v6 on v5

--- a/solution.py
+++ b/solution.py
@@ -28,15 +28,58 @@
 STAGE2 = BF16
 
 
+def factor(work, inverse):
+    rank = work.shape[0]
+    lane = lax.broadcasted_iota(jnp.int32, (PANEL, rank), 1)
+    row = lax.broadcasted_iota(jnp.int32, (PANEL, rank), 0)
+    wide = lax.broadcasted_iota(jnp.int32, (rank, rank), 1)
+    for p in range(rank // PANEL):
+        first = p * PANEL
+        rest = first + PANEL
+        at = lane - first
+        lower = work[first:rest]
+        solved = lower
+        cols = [
+            jnp.broadcast_to(lower[:, first + j:first + j + 1], (PANEL, rank)) for j in range(PANEL)
+        ]
+        roots = jnp.ones((PANEL, rank), F32)
+        for j in range(PANEL):
+            own = row == j
+            pivot = jnp.broadcast_to(cols[j][j:j + 1], (PANEL, rank))
+            roots = jnp.where(own, pivot, roots)
+            scaled = 1.0 / pivot
+            mult = cols[j] * scaled
+            for i in range(j + 1, PANEL):
+                line = jnp.broadcast_to(cols[i][j:j + 1], (PANEL, rank))
+                cols[i] = jnp.where(own, line * scaled, cols[i] - mult * line)
+            line = jnp.broadcast_to(solved[j:j + 1], (PANEL, rank))
+            pick = jnp.where(own, scaled, -mult)
+            solved = jnp.where(at == j, pick, jnp.where(own, line * scaled, solved - mult * line))
+            below = jnp.where(row > j, mult, 0.0)
+            updated = lower - below * lower[j:j + 1]
+            lower = jnp.where((at == j) & (row > j), -mult, updated)
+        lower = jnp.where(at < row, lower, jnp.where(at == row, 1.0, 0.0))
+        inverse[first:rest] = lower / jnp.sqrt(roots)
+        if rest < rank:
+            parts = [jnp.zeros((first, rank), F32)] if first else []
+            parts += [solved, jnp.zeros((rank - rest, rank), F32)]
+            left = work[rest:]
+            step = jnp.dot(
+                left, jnp.concatenate(parts, axis=0), precision=HIGHEST, preferred_element_type=F32
+            )
+            inside = (wide[rest:] >= first) & (wide[rest:] < rest)
+            work[rest:] = jnp.where(inside, 0.0, left) - step
+
+
 def reduce_kernel(
-    act_in, grads_in, omega, rows_out, gram_out,
-    act, grads, act2, act_t, other, sk, ext, slab, send1, recv1, send2, recv2,
+    act_in, grads_in, omega_in, out,
+    omega, act, grads, act2, act_t, other, sk, ext, slab, send1, recv1, send2, recv2,
     send3, recv3, send4, recv4, send6, recv9, send8, recv8, send9, recv10, mine,
     part2, recv5, rolled,
-    gram, recv6, part, recv7, full, ssem, rsem, lsem,
+    gram, recv6, part, recv7, full, rows_in, work, inverse, inverse_in, ssem, rsem, lsem, *, scale,
 ):
     layers, _, frames, height, width, channels = act_in.shape
-    rank = omega.shape[1]
+    rank = omega_in.shape[1]
     dp, space = lax.axis_index("dp"), lax.axis_index("space")
     y, core = dp // 2, dp % 2
     x, z = space // RING, space % RING
@@ -68,15 +111,17 @@
         pltpu.make_async_copy(grads_in.at[1 - core], grads.at[0], lsem.at[0]),
         pltpu.make_async_copy(grads_in.at[core], grads.at[1], lsem.at[1]),
         pltpu.make_async_copy(act_in.at[core], act, lsem.at[2]),
+        pltpu.make_async_copy(omega_in, omega, lsem.at[3]),
     ]
-    for copy in loads:
-        copy.start()
+    for n in (3, 0, 1, 2):
+        loads[n].start()
 
     def sketch(n, h):
         flat = grads[n, 0, :, h].reshape(frames * width, channels)
         value = jnp.dot(flat, omega[...], preferred_element_type=F32).astype(BF16)
         return value.reshape(frames, width, rank)
 
+    loads[3].wait()
     loads[0].wait()
     for h in range(height):
         other[h] = sketch(0, h)
@@ -310,8 +355,7 @@
     gram[...] = product.reshape(spaces, rank // spaces, rank)
 
     copies = [send(gram.at[to["space"]], recv6.at[n], to) for n, to in enumerate(plane)]
-    rows_copy = send(rolled.at[1 - core], rows_out.at[core], partner)
-    rows_out[core] = rolled[core]
+    rows_copy = send(rolled.at[1 - core], rows_in, partner)
     value = gram[space]
     for n, copy in enumerate(copies):
         copy.wait_recv()
@@ -326,63 +370,25 @@
     copies = [send(part.at[1], full.at[space], to) for to in plane]
     for copy in copies:
         copy.wait_recv()
-    copy = send(full, gram_out.at[core], partner)
-    gram_out[core] = full[...]
+
+    work[...] = full[...].reshape(rank, rank)
+    factor(work, inverse)
+    copy = send(inverse, inverse_in, partner)
+
+    def solve(rows, lower):
+        value = lax.dot_general(
+            rows, lower, (((1,), (1,)), ((), ())), precision=HIGHEST, preferred_element_type=F32
+        )
+        return (value * scale)[:OWN]
+
+    near = solve(rolled[core], inverse[...])
+    rows_copy.wait_recv()
     copy.wait_recv()
-    rows_copy.wait_recv()
+    far = solve(rows_in[...], inverse_in[...])
+    out[:, 0] = jnp.where(core == 0, near, far)
+    out[:, 1] = jnp.where(core == 0, far, near)
     for copy in sent:
         copy.wait_send()
-
-
-def factor_kernel(rows, gram, out, work, inverse, *, scale):
-    layers, rank, _ = gram.shape
-    lane = lax.broadcasted_iota(jnp.int32, (PANEL, rank), 1)
-    row = lax.broadcasted_iota(jnp.int32, (PANEL, rank), 0)
-    wide = lax.broadcasted_iota(jnp.int32, (rank, rank), 1)
-    work[...] = gram[...]
-    for p in range(rank // PANEL):
-        first = p * PANEL
-        rest = first + PANEL
-        at = lane - first
-        for l in range(layers):
-            lower = work[l, first:rest]
-            solved = lower
-            cols = [
-                jnp.broadcast_to(lower[:, first + j:first + j + 1], (PANEL, rank)) for j in range(PANEL)
-            ]
-            roots = jnp.ones((PANEL, rank), F32)
-            for j in range(PANEL):
-                own = row == j
-                pivot = jnp.broadcast_to(cols[j][j:j + 1], (PANEL, rank))
-                roots = jnp.where(own, pivot, roots)
-                scaled = 1.0 / pivot
-                mult = cols[j] * scaled
-                for i in range(j + 1, PANEL):
-                    line = jnp.broadcast_to(cols[i][j:j + 1], (PANEL, rank))
-                    cols[i] = jnp.where(own, line * scaled, cols[i] - mult * line)
-                line = jnp.broadcast_to(solved[j:j + 1], (PANEL, rank))
-                pick = jnp.where(own, scaled, -mult)
-                solved = jnp.where(at == j, pick, jnp.where(own, line * scaled, solved - mult * line))
-                below = jnp.where(row > j, mult, 0.0)
-                updated = lower - below * lower[j:j + 1]
-                lower = jnp.where((at == j) & (row > j), -mult, updated)
-            lower = jnp.where(at < row, lower, jnp.where(at == row, 1.0, 0.0))
-            inverse[l, first:rest] = lower / jnp.sqrt(roots)
-            if rest < rank:
-                parts = [jnp.zeros((first, rank), F32)] if first else []
-                parts += [solved, jnp.zeros((rank - rest, rank), F32)]
-                left = work[l, rest:]
-                step = jnp.dot(
-                    left, jnp.concatenate(parts, axis=0), precision=HIGHEST, preferred_element_type=F32
-                )
-                inside = (wide[rest:] >= first) & (wide[rest:] < rest)
-                work[l, rest:] = jnp.where(inside, 0.0, left) - step
-    for l in range(layers):
-        value = lax.dot_general(
-            rows[l], inverse[l], (((1,), (1,)), ((), ())),
-            precision=HIGHEST, preferred_element_type=F32,
-        )
-        out[:, l] = (value * scale)[:OWN]
 
 
 def shards(activations, out_grads, omega):
@@ -392,16 +398,14 @@
     vmem = pl.BlockSpec(memory_space=pltpu.VMEM)
     blocks, fewer = (RING, WIN, rank), (RING - 1, WIN, rank)
     gram_blocks = (RING * RING, rank // (RING * RING), rank)
-    rows, gram = pl.pallas_call(
-        reduce_kernel,
-        name="reduce",
-        out_shape=(
-            jax.ShapeDtypeStruct((layers, WIN, rank), F32),
-            jax.ShapeDtypeStruct((layers,) + gram_blocks, F32),
-        ),
-        in_specs=[pl.BlockSpec(memory_space=pl.ANY)] * 2 + [vmem],
-        out_specs=(vmem, vmem),
+    basis = pl.pallas_call(
+        functools.partial(reduce_kernel, scale=math.sqrt(27 * channels)),
+        name="refresh",
+        out_shape=jax.ShapeDtypeStruct((OWN, layers, rank), F32),
+        in_specs=[pl.BlockSpec(memory_space=pltpu.HBM)] * 3,
+        out_specs=vmem,
         scratch_shapes=[
+            pltpu.VMEM(omega.shape, BF16),
             pltpu.VMEM(activations.shape[1:], BF16),
             pltpu.VMEM(activations.shape, BF16),
             pltpu.VMEM(activations.shape[1:], BF16),
@@ -433,25 +437,18 @@
             pltpu.VMEM((2,) + gram_blocks[1:], F32),
             pltpu.VMEM((RING - 1,) + gram_blocks[1:], F32),
             pltpu.VMEM(gram_blocks, F32),
+            pltpu.VMEM((WIN, rank), F32),
+            pltpu.VMEM((rank, rank), F32),
+            pltpu.VMEM((rank, rank), F32),
+            pltpu.VMEM((rank, rank), F32),
             pltpu.SemaphoreType.DMA((112,)),
             pltpu.SemaphoreType.DMA((112,)),
-            pltpu.SemaphoreType.DMA((3,)),
+            pltpu.SemaphoreType.DMA((4,)),
         ],
         compiler_params=pltpu.CompilerParams(
-            collective_id=0, has_side_effects=True, vmem_limit_bytes=60 * 2**20
+            collective_id=0, has_side_effects=True, vmem_limit_bytes=13721 * 4096
         ),
     )(activations, out_grads, omega)
-    basis = pl.pallas_call(
-        functools.partial(factor_kernel, scale=math.sqrt(27 * channels)),
-        name="factor",
-        out_shape=jax.ShapeDtypeStruct((OWN, layers, rank), F32),
-        in_specs=[vmem] * 2,
-        out_specs=vmem,
-        scratch_shapes=[
-            pltpu.VMEM((layers, rank, rank), F32),
-            pltpu.VMEM((layers, rank, rank), F32),
-        ],
-    )(rows, gram.reshape(layers, rank, rank))
     return jnp.transpose(basis, (1, 0, 2))
 
 

time: 74.1 us -> 70.1 us (0.946)
  Pallas kernels: 74 us -> 69.3 us
    pallas_call x2 -> x1, Pallas kernels: 74 us -> 69.3 us  [shards(): pl.pallas_call(functools.partial(reduce_kernel, scale=math.sqrt(27 * chan...]
where the time goes in v6:
time: 70.1 us; the launch traced here: 70 us
  Pallas kernels  69.3 us (99%)
    pallas_call x1, Pallas kernels, shards(): pl.pallas_call(functools.partial(reduce_kernel, scale=math.sqrt(27 * chan...  69.3 us

profile of v6, /device:TPU:1, one launch (start us, length us, event | category | flops | bytes accessed | tf_op | source)
XLA Modules:
  0.0 70.0 jit_solution(12097210406837359650)
XLA Ops:
  0.0 69.3 %refresh.1 = f32[162,2,128]{2,1,0:T(2,128)S(1)} custom-call(bf16[2,1,8,2,32,768]{5,4,3,2,1,0:T(8,128)(2,1)} %act_in.1, bf16[2,1,8,2,32,768]{5,4,3,2,1,0:T(8,128)(2,1)} %grads_in.1, bf16[768,128]{1,0:T(8,128)(2,1)} %omega_in.1), custom_call_target="tpu_custom_call" | custom-call | tf_op jit(solution)/shard_map/refresh/pallas_call | solution.py:401
  69.3 0.7 copy.5

commit v7 on v6

--- a/solution.py
+++ b/solution.py
@@ -19,6 +19,7 @@
 ORDER = (2, 1, 3, 0)
 CHUNKS = [(r, e) for r in ORDER for e in (0, 1)]
 PANEL = 16
+EARLY = ORDER
 SCHEDULE = (
     "C0", "S0", "C1", "S1", "T0", "T1", "C2", "S2", "C3", "S3", "M0", "P1", "P0", "M1", "C4", "S4",
     "T2", "T4", "M2", "P2", "C5", "S5", "P3", "C6", "F1", "M3", "F0", "P4", "M4", "C7", "S7", "T5",
@@ -187,11 +188,6 @@
         extend(1, h)
     act_copy.wait_recv()
     transpose(1, act2)
-    for slot in range(2):
-        for copy, h in zip(halo_copies[slot], outer):
-            copy.wait_recv()
-            extend(slot, h)
-
     depth = 2 * height * frames * width
 
     def compute(r, pairs):
@@ -202,7 +198,9 @@
             a, b, c = k // 9, k // 3 % 3, k % 3
             return ext[c, :, pl.ds(2 - b, height), pl.ds(2 - a, frames)].reshape(depth, rank)
 
-        def pair(i, _):
+        early = (y + r + 2) % RING if r in EARLY else SLAB
+
+        def pair(i):
             both = jnp.concatenate([columns(2 * i), columns(2 * i + 1)], axis=1)
             for m in range(3):
                 rows = channels // 3
@@ -210,9 +208,26 @@
                 for s in range(2):
                     at = pl.multiple_of((2 * i + s) * channels + m * rows, rows)
                     slab[r, pl.ds(at, rows)] = value[:, s * rank:(s + 1) * rank]
+
+        def step(i, _):
+            @pl.when(i != early)
+            def _():
+                pair(i)
+
             return 0
 
-        lax.fori_loop(pairs[0], pairs[1], pair, 0)
+        if pairs is None:
+            pair(early)
+        else:
+            lax.fori_loop(pairs[0], pairs[1], step, 0)
+
+    for r in EARLY:
+        compute(r, None)
+
+    for slot in range(2):
+        for copy, h in zip(halo_copies[slot], outer):
+            copy.wait_recv()
+            extend(slot, h)
 
     def window(r, e, mine, o):
         owner = (y + r) % RING * 2 + e

time: 70.1 us -> 68.9 us (0.983)
  Pallas kernels: 69.3 us -> 68.1 us
    pallas_call x1, Pallas kernels: 69.3 us -> 68.1 us  [shards(): pl.pallas_call(functools.partial(reduce_kernel, scale=math.sqrt(27 * chan...]
where the time goes in v7:
time: 68.9 us; the launch traced here: 68.7 us
  Pallas kernels  68.1 us (99%)
    pallas_call x1, Pallas kernels, shards(): pl.pallas_call(functools.partial(reduce_kernel, scale=math.sqrt(27 * chan...  68.1 us

profile of v7, /device:TPU:1, one launch (start us, length us, event | category | flops | bytes accessed | tf_op | source)
XLA Modules:
  0.0 68.7 jit_solution(14547186713408193623)
XLA Ops:
  0.0 68.1 %refresh.1 = f32[162,2,128]{2,1,0:T(2,128)S(1)} custom-call(bf16[2,1,8,2,32,768]{5,4,3,2,1,0:T(8,128)(2,1)} %act_in.1, bf16[2,1,8,2,32,768]{5,4,3,2,1,0:T(8,128)(2,1)} %grads_in.1, bf16[768,128]{1,0:T(8,128)(2,1)} %omega_in.1), custom_call_target="tpu_custom_call" | custom-call | tf_op jit(solution)/shard_map/refresh/pallas_call | solution.py:416
  68.1 0.7 copy.5

commit v8 on v7

--- a/solution.py
+++ b/solution.py
@@ -97,6 +97,7 @@
     spaces = RING * RING
     below, above = (space + 1) % spaces, (space + spaces - 1) % spaces
     turns = [(a, b) for a in range(RING) for b in range(RING) if a or b]
+    turns.sort(key=lambda t: -(min(t[0], RING - t[0]) + min(t[1], RING - t[1])))
     plane = [
         {"dp": dp, "space": (x + a) % RING * RING + (z + b) % RING} for a, b in turns
     ]
@@ -143,6 +144,12 @@
         sent.append(copy)
         return copy
 
+    def settle(last):
+        while settled[0] < last:
+            sent[settled[0]].wait_send()
+            settled[0] += 1
+
+    settled = [0]
     halo_copies = [
         [
             send(sk.at[0, height], sk.at[0, 0], {"dp": dp, "space": below}),
@@ -371,24 +378,28 @@
 
     copies = [send(gram.at[to["space"]], recv6.at[n], to) for n, to in enumerate(plane)]
     rows_copy = send(rolled.at[1 - core], rows_in, partner)
+    settle(len(sent) - len(copies) - 1)
     value = gram[space]
-    for n, copy in enumerate(copies):
+    for n, copy in reversed(list(enumerate(copies))):
         copy.wait_recv()
         value = value + recv6[n]
     part[0] = value
     copies = [send(part.at[0], recv7.at[n], to) for n, to in enumerate(stack)]
+    settle(len(sent) - len(copies))
     for n, copy in enumerate(copies):
         copy.wait_recv()
         value = value + recv7[n]
     part[1] = value
     full[space] = value
     copies = [send(part.at[1], full.at[space], to) for to in plane]
+    settle(len(sent) - len(copies))
     for copy in copies:
         copy.wait_recv()
 
     work[...] = full[...].reshape(rank, rank)
     factor(work, inverse)
     copy = send(inverse, inverse_in, partner)
+    settle(len(sent) - 1)
 
     def solve(rows, lower):
         value = lax.dot_general(
@@ -402,8 +413,7 @@
     far = solve(rows_in[...], inverse_in[...])
     out[:, 0] = jnp.where(core == 0, near, far)
     out[:, 1] = jnp.where(core == 0, far, near)
-    for copy in sent:
-        copy.wait_send()
+    settle(len(sent))
 
 
 def shards(activations, out_grads, omega):

time: 68.9 us -> 68.2 us (0.990)
  Pallas kernels: 68.1 us -> 67.4 us
    pallas_call x1, Pallas kernels: 68.1 us -> 67.4 us  [shards(): pl.pallas_call(functools.partial(reduce_kernel, scale=math.sqrt(27 * chan...]
where the time goes in v8:
time: 68.2 us; the launch traced here: 68 us
  Pallas kernels  67.4 us (99%)
    pallas_call x1, Pallas kernels, shards(): pl.pallas_call(functools.partial(reduce_kernel, scale=math.sqrt(27 * chan...  67.4 us

profile of v8, /device:TPU:1, one launch (start us, length us, event | category | flops | bytes accessed | tf_op | source)
XLA Modules:
  0.0 68.0 jit_solution(6449073357649943934)
XLA Ops:
  0.0 67.4 %refresh.1 = f32[162,2,128]{2,1,0:T(2,128)S(1)} custom-call(bf16[2,1,8,2,32,768]{5,4,3,2,1,0:T(8,128)(2,1)} %act_in.1, bf16[2,1,8,2,32,768]{5,4,3,2,1,0:T(8,128)(2,1)} %grads_in.1, bf16[768,128]{1,0:T(8,128)(2,1)} %omega_in.1), custom_call_target="tpu_custom_call" | custom-call | tf_op jit(solution)/shard_map/refresh/pallas_call | solution.py:426
  67.4 0.7 copy.5

commit v9 on v8

--- a/solution.py
+++ b/solution.py
@@ -101,7 +101,7 @@
     plane = [
         {"dp": dp, "space": (x + a) % RING * RING + (z + b) % RING} for a, b in turns
     ]
-    stack = [along("y", j) for j in (1, 2, 3)]
+    stack = [along("y", j) for j in (2, 1, 3)]
     crossed = [{"dp": other_dp, "space": below}, {"dp": other_dp, "space": above}]
     peers = [partner] + crossed + plane + stack
 
@@ -337,7 +337,7 @@
         elif r == 0:
             turn3[e] = [
                 send(send9.at[e, (first_at[e] + j) % RING], recv10.at[e, j - 1], along(first_axis[e], j))
-                for j in (1, 2, 3)
+                for j in (2, 1, 3)
             ]
         else:
             turn2.setdefault(e, []).append(send(send8.at[e, s], recv8.at[e, s], along("y", r)))
@@ -348,7 +348,7 @@
         part2[e, 0] = add([mine[e, first_at[e]], recv10[e, 0], recv10[e, 1], recv10[e, 2]])
         step5[e] = [
             send(part2.at[e, (last_at[e] + j) % RING], recv5.at[e, j - 1], along(last_axis[e], j))
-            for j in (1, 2, 3)
+            for j in (2, 1, 3)
         ]
 
     for entry in SCHEDULE:

time: 68.2 us -> 67.4 us (0.988)
  Pallas kernels: 67.4 us -> 66.6 us
    pallas_call x1, Pallas kernels: 67.4 us -> 66.6 us  [shards(): pl.pallas_call(functools.partial(reduce_kernel, scale=math.sqrt(27 * chan...]
where the time goes in v9:
time: 67.4 us; the launch traced here: 67.3 us
  Pallas kernels  66.6 us (99%)
    pallas_call x1, Pallas kernels, shards(): pl.pallas_call(functools.partial(reduce_kernel, scale=math.sqrt(27 * chan...  66.6 us

profile of v9, /device:TPU:1, one launch (start us, length us, event | category | flops | bytes accessed | tf_op | source)
XLA Modules:
  0.0 67.3 jit_solution(396391516252255181)
XLA Ops:
  0.0 66.6 %refresh.1 = f32[162,2,128]{2,1,0:T(2,128)S(1)} custom-call(bf16[2,1,8,2,32,768]{5,4,3,2,1,0:T(8,128)(2,1)} %act_in.1, bf16[2,1,8,2,32,768]{5,4,3,2,1,0:T(8,128)(2,1)} %grads_in.1, bf16[768,128]{1,0:T(8,128)(2,1)} %omega_in.1), custom_call_target="tpu_custom_call" | custom-call | tf_op jit(solution)/shard_map/refresh/pallas_call | solution.py:426
  66.7 0.7 copy.5
